TPU v7x, 32 devices: a whole 2x2x4 slice. The times are simulated.
32 devices in a mesh: flow: 8 (over z, x), cross: 4 (over y, core).
Axes of the slice: x: 2, y: 2, z: 4, core: 2. Of those that a mesh axis runs over, the one named last changes fastest.
Arguments:
- right_side: float32 [8, 256, 320], P('flow', 'cross'), may hold values from -6 to 6
- old_state: float32 [8, 256, 320], P('flow', 'cross'), may hold values from -6 to 6
- block_inverse: bfloat16 [8, 256, 320, 320], P('flow', 'cross'), as said below
- flux_jacobian: float32 [8, 256, 4, 25], P('flow', 'cross'), may hold values from -1.35 to 1.35, as said below
- face_lift: float32 [4, 64, 64], replicated, may hold values from -0.75 to 0.75
- upstream: int32 [8, 256], P('flow', 'cross'), may hold values from 0 to 255, as said below
- downstream: int32 [8, 256], P('flow', 'cross'), may hold values from 0 to 255, as said below
- live_counts: int32 [8, 4], P('flow', 'cross'), may hold values from 32 to 64, as said below
Outputs:
- half_sweep: float32 [8, 256, 320], P('flow', 'cross')
- full_sweep: float32 [8, 256, 320], P('flow', 'cross')
Inputs may be any that keep to these rules, and one draw needn't show every extreme that they name: In each layer the upstream slots of an aligned block of 4 slots are a permutation of that same block's slots. downstream[l] is the inverse permutation of upstream[l + 1] (of upstream[0] for the last layer): upstream[l + 1, downstream[l, e]] = e. `live_counts`: slots at or beyond the count in their run hold no element; some run is full. `block_inverse`: each block is the sum of a multiple of the identity and a full dense part. `flux_jacobian`: entries are centred; those of the upstream and downstream faces are of order 0.45, those of the left and right faces of order 0.27.
All inputs are finite; a program needn't handle non-finite values.
Results may differ from a plain program's by a relative error of at most 0.017.
Values sent between devices are 32-bit elements; how exact they have to be, the bound alone decides.
A program may use at most 64 MiB of HBM per device.

v0:
```python
import jax
import jax.numpy as jnp
from jax import lax
from jax.sharding import PartitionSpec as P

HIGHEST_PRECISION = lax.Precision.HIGHEST


def passed_along(block, axis, distance):
    devices = range(lax.axis_size(axis))
    route = [(i - distance, i) for i in devices if i - distance in devices]
    return lax.ppermute(block, axis, route)


def extended(cells, sides, width):
    for axis, dim in sides:
        count = lax.axis_size(axis)
        ends = count - 1
        head = lax.slice_in_dim(cells, 0, width, axis=dim)
        tail = lax.slice_in_dim(cells, cells.shape[dim] - width, cells.shape[dim], axis=dim)
        cells = jnp.concatenate(
            [
                lax.ppermute(tail, axis, [(i, (i + 1) % count) for i in range(ends)]),
                cells,
                lax.ppermute(head, axis, [((i + 1) % count, i) for i in range(ends)]),
            ],
            axis=dim,
        )
    return cells


def couple(values, lift, jacobian_face):
    spread = jnp.einsum("...vc,bc->...vb", values, lift, precision=HIGHEST_PRECISION)
    mixing = jacobian_face.reshape(jacobian_face.shape[:-1] + (5, 5))
    return jnp.einsum("...uv,...vb->...ub", mixing, spread, precision=HIGHEST_PRECISION)


def solve_blocks(inverse, residual, live):
    flat = residual.reshape(residual.shape[:-2] + (-1,)).astype(jnp.bfloat16)
    solved = jnp.einsum("...ij,...j->...i", inverse, flat, preferred_element_type=jnp.float32)
    return (solved * live[..., None]).reshape(residual.shape)


def group_slices(arrays):
    return [item for item in arrays]


def forward_chain(fixed_fwd, block_inverse, jacobian_up, lift_up, up_local, live, group_count):
    layer_count, elem_count = up_local.shape
    group_width = elem_count // group_count
    flow_size = lax.axis_size("flow")
    flow_place = lax.axis_index("flow")
    block_shape = (layer_count, group_width) + fixed_fwd.shape[2:]

    def forward_run_group(inbound, start_elem):
        fixed_part, inverse_part, jacobian_part, index_part, live_part = group_slices(
            (fixed_fwd, block_inverse, jacobian_up, up_local, live)
        )
        index_part = index_part - start_elem
        nearest = inbound[index_part[0]]
        solved = solve_blocks(
            inverse_part[0],
            fixed_part[0] - couple(nearest, lift_up, jacobian_part[0]),
            live_part[0],
        )
        solved_rows = [solved]
        return (jnp.stack(solved_rows), solved)

    def forward_skip_group(inbound, start_elem):
        return (jnp.zeros(block_shape, jnp.float32), jnp.zeros_like(inbound))

    def forward_run_section(step_index, carried):
        outbound, gathered, received = carried
        inbound = passed_along(outbound, "flow", 1)
        group_index = step_index - flow_place
        start_elem = jnp.clip(group_index, 0, group_count - 1) * group_width
        usable = (group_index >= 0) & (group_index < group_count)
        solved_block, last_layer = lax.cond(
            usable, forward_run_group, forward_skip_group, inbound, start_elem
        )
        updated = lax.dynamic_update_slice_in_dim(gathered, solved_block, start_elem, 1)
        return (
            last_layer,
            jnp.where(usable, updated, gathered),
            jnp.where(usable, inbound, received),
        )

    initial = (
        jnp.zeros((group_width,) + fixed_fwd.shape[2:], jnp.float32),
        jnp.zeros_like(fixed_fwd),
        jnp.zeros_like(fixed_fwd[0]),
    )
    _, result, received = lax.fori_loop(
        0, flow_size + group_count - 1, forward_run_section, initial
    )
    return (result, received)


def backward_chain(
    fixed_bwd, block_inverse, jacobian_down, lift_down, down_local, live, group_count
):
    layer_count, elem_count = down_local.shape
    group_width = elem_count // group_count
    flow_size = lax.axis_size("flow")
    flow_place = lax.axis_index("flow")
    block_shape = (layer_count, group_width) + fixed_bwd.shape[2:]

    def backward_run_group(inbound, start_elem):
        fixed_part, inverse_part, jacobian_part, index_part, live_part = group_slices(
            (fixed_bwd, block_inverse, jacobian_down, down_local, live)
        )
        index_part = index_part - start_elem
        later = inbound
        solved_rows = [None] * layer_count
        for layer_pos in reversed(range(layer_count)):
            nearest = later[index_part[layer_pos]]
            solved = solve_blocks(
                inverse_part[layer_pos],
                fixed_part[layer_pos] - couple(nearest, lift_down, jacobian_part[layer_pos]),
                live_part[layer_pos],
            )
            solved_rows[layer_pos] = solved
            later = solved
        return (jnp.stack(solved_rows), later)

    def backward_skip_group(inbound, start_elem):
        return (jnp.zeros(block_shape, jnp.float32), jnp.zeros_like(inbound))

    def backward_run_section(step_index, carried):
        outbound, gathered = carried
        inbound = passed_along(outbound, "flow", -1)
        group_index = step_index - (flow_size - 1 - flow_place)
        start_elem = jnp.clip(group_index, 0, group_count - 1) * group_width
        usable = (group_index >= 0) & (group_index < group_count)
        solved_block, first_layer = lax.cond(
            usable, backward_run_group, backward_skip_group, inbound, start_elem
        )
        updated = lax.dynamic_update_slice_in_dim(gathered, solved_block, start_elem, 1)
        return (first_layer, jnp.where(usable, updated, gathered))

    initial = (
        jnp.zeros((group_width,) + fixed_bwd.shape[2:], jnp.float32),
        jnp.zeros_like(fixed_bwd),
    )
    _, result = lax.fori_loop(0, flow_size + group_count - 1, backward_run_section, initial)
    return result


def per_device(
    right_side,
    old_state,
    block_inverse,
    flux_jacobian,
    face_lift,
    upstream,
    downstream,
    live_counts,
):
    layer_count, elem_count, unknowns = right_side.shape
    grid_shape = (layer_count, elem_count, 5, unknowns // 5)
    source = right_side.reshape(grid_shape)
    slot_index = jnp.arange(elem_count, dtype=jnp.int32)
    live = (slot_index[None, :] < live_counts).astype(jnp.float32)
    up_local = upstream % elem_count
    down_local = downstream % elem_count
    group_count = 1
    state_old = old_state.reshape(grid_shape) * live[:, :, None, None]
    padded_old = extended(state_old, (("cross", 1),), 1)
    next_first = passed_along(state_old[0], "flow", -1)
    following = jnp.concatenate([state_old[1:], next_first[None]], 0)
    down_old = jnp.take_along_axis(following, down_local[:, :, None, None], axis=1)
    fixed_fwd = (
        source
        - couple(down_old, face_lift[1], flux_jacobian[:, :, 1])
        - couple(padded_old[:, :-2], face_lift[2], flux_jacobian[:, :, 2])
        - couple(padded_old[:, 2:], face_lift[3], flux_jacobian[:, :, 3])
    )
    half_state, received = forward_chain(
        fixed_fwd, block_inverse, flux_jacobian[:, :, 0], face_lift[0], up_local, live, group_count
    )
    padded_half = extended(half_state, (("cross", 1),), 1)
    earlier = jnp.concatenate([received[None], half_state[:-1]], 0)
    up_new = jnp.take_along_axis(earlier, up_local[:, :, None, None], axis=1)
    fixed_bwd = (
        source
        - couple(up_new, face_lift[0], flux_jacobian[:, :, 0])
        - couple(padded_half[:, :-2], face_lift[2], flux_jacobian[:, :, 2])
        - couple(padded_half[:, 2:], face_lift[3], flux_jacobian[:, :, 3])
    )
    full_state = backward_chain(
        fixed_bwd,
        block_inverse,
        flux_jacobian[:, :, 1],
        face_lift[1],
        down_local,
        live,
        group_count,
    )
    return (half_state.reshape(right_side.shape), full_state.reshape(right_side.shape))


def solution(mesh):
    in_specs = (
        P("flow", "cross", None),
        P("flow", "cross", None),
        P("flow", "cross", None, None),
        P("flow", "cross", None, None),
        P(),
        P("flow", "cross"),
        P("flow", "cross"),
        P("flow", "cross"),
    )
    out_specs = (P("flow", "cross", None), P("flow", "cross", None))
    return jax.shard_map(
        per_device, mesh=mesh, in_specs=in_specs, out_specs=out_specs, check_vma=False
    )
```

profile of v0, /device:TPU:0, one launch (start us, length us, event | category | flops | bytes accessed | tf_op | source)
XLA Modules:
  0.0 385.0 jit_solution(11802459803939563711)
XLA Ops:
  4.0 2.4 collective-permute-start.3
  19.6 135.1 %while.36 = (s32[]{:T(128)}, f32[64,5,64]{0,2,1:T(8,128)}, f32[1,64,5,64]{1,3,2,0:T(8,128)S(1)}, f32[64,5,64]{2,1,0:T(8,128)S(1)}, s32[]{:T(128)}, /*index=5*/f3...) while((s32[]{:T(128)}, f32[64,5,64]{0,2,1:T(8,128)}, ...), condition=%wide.region_3.5_spmd.clone, body=%wide.region_0.4_spmd.clone.sunk | while | flops 36763016 | bytes 15701076 | solution.py:93
  20.7 4.9 %collective-permute-start = (f32[64,5,64]{2,1,0:T(8,128)S(1)}, f32[64,5,64]{2,1,0:T(8,128)S(1)}, u32[]{:S(2)}, u32[]{:S(2)}) collective-permute-start(f32[64,5,64]{2,1,0:T(8,128)S(1)} %copy.156), channel_id=1, source_target_pairs={{0,4},{4,8},{8,12},{12,16},{16,20},{20,24},{24,28},{1,5},{5,9},{9,... | collective-permute-start | bytes 245768 | tf_op jit(solution)/shard_map/while/body/eval_jaxpr/ppermute | solution.py:12
  26.2 3.9 %collective-permute-done = f32[64,5,64]{2,1,0:T(8,128)S(1)} collective-permute-done((f32[64,5,64]{2,1,0:T(8,128)S(1)}, f32[64,5,64]{2,1,0:T(8,128)S(1)}, u32[]{:S(2)}, u32[]{:S(2)}) %collective-permute-start) | collective-permute-done | bytes 81952 | tf_op jit(solution)/shard_map/while/body/eval_jaxpr/ppermute | solution.py:12
  30.2 11.6 %conditional.6 = (f32[1,64,5,64]{1,3,2,0:T(8,128)}, f32[64,5,64]{0,2,1:T(8,128)}) conditional(s32[]{:T(128)} %convert_element_type.69, () %tuple.115, (f32[1,64,5,64]{3,2,1,0:T(8,128)S(1)}, s32[]{:T(128)}, s32[1,64]{1,0:T(1,128)S(1)}, f32[64,5,64]{2,1,0:T(8,128)S(1)}, f32[64,64]{1,0:T(8,128)S(1)}, /*index=5*/f32[1,64,1,25]{1,3,2,0:T(8,128)S(1)}, ...), branch_computations={%region_1.2_spmd, %region_2.3_spmd} | conditional | flops 36680964 | bytes 14717496 | solution.py:78
  32.2 7.1 %multiply_reduce_fusion = f32[64,320]{1,0:T(8,128)S(1)} fusion(f32[64,320]{1,0:T(8,128)S(1)} %copy.124, bf16[1,64,320,320]{3,2,1,0:T(8,128)(2,1)} %get-tuple-element.489), kind=kLoop, calls=%fused_computation.6 | loop fusion | flops 19640320 | bytes 13271040 | tf_op jit(solution)/shard_map/while/body/eval_jaxpr/cond
  40.1 1.6 copy.161
  43.9 1.3 collective-permute-start
  45.9 4.4 %collective-permute-done = f32[64,5,64]{2,1,0:T(8,128)S(1)} collective-permute-done((f32[64,5,64]{2,1,0:T(8,128)S(1)}, f32[64,5,64]{2,1,0:T(8,128)S(1)}, u32[]{:S(2)}, u32[]{:S(2)}) %collective-permute-start) | collective-permute-done | bytes 81952 | tf_op jit(solution)/shard_map/while/body/eval_jaxpr/ppermute | solution.py:12
  50.3 1.3 conditional.6
  52.9 15.5 %collective-permute-start = (f32[64,5,64]{2,1,0:T(8,128)S(1)}, f32[64,5,64]{2,1,0:T(8,128)S(1)}, u32[]{:S(2)}, u32[]{:S(2)}) collective-permute-start(f32[64,5,64]{2,1,0:T(8,128)S(1)} %copy.156), channel_id=1, source_target_pairs={{0,4},{4,8},{8,12},{12,16},{16,20},{20,24},{24,28},{1,5},{5,9},{9,... | collective-permute-start | bytes 245768 | tf_op jit(solution)/shard_map/while/body/eval_jaxpr/ppermute | solution.py:12
  69.1 5.7 %collective-permute-done = f32[64,5,64]{2,1,0:T(8,128)S(1)} collective-permute-done((f32[64,5,64]{2,1,0:T(8,128)S(1)}, f32[64,5,64]{2,1,0:T(8,128)S(1)}, u32[]{:S(2)}, u32[]{:S(2)}) %collective-permute-start) | collective-permute-done | bytes 81952 | tf_op jit(solution)/shard_map/while/body/eval_jaxpr/ppermute | solution.py:12
  74.8 1.3 conditional.6
  77.4 4.4 %collective-permute-start = (f32[64,5,64]{2,1,0:T(8,128)S(1)}, f32[64,5,64]{2,1,0:T(8,128)S(1)}, u32[]{:S(2)}, u32[]{:S(2)}) collective-permute-start(f32[64,5,64]{2,1,0:T(8,128)S(1)} %copy.156), channel_id=1, source_target_pairs={{0,4},{4,8},{8,12},{12,16},{16,20},{20,24},{24,28},{1,5},{5,9},{9,... | collective-permute-start | bytes 245768 | tf_op jit(solution)/shard_map/while/body/eval_jaxpr/ppermute | solution.py:12
  82.5 5.2 %collective-permute-done = f32[64,5,64]{2,1,0:T(8,128)S(1)} collective-permute-done((f32[64,5,64]{2,1,0:T(8,128)S(1)}, f32[64,5,64]{2,1,0:T(8,128)S(1)}, u32[]{:S(2)}, u32[]{:S(2)}) %collective-permute-start) | collective-permute-done | bytes 81952 | tf_op jit(solution)/shard_map/while/body/eval_jaxpr/ppermute | solution.py:12
  87.7 1.3 conditional.6
  90.3 14.0 %collective-permute-start = (f32[64,5,64]{2,1,0:T(8,128)S(1)}, f32[64,5,64]{2,1,0:T(8,128)S(1)}, u32[]{:S(2)}, u32[]{:S(2)}) collective-permute-start(f32[64,5,64]{2,1,0:T(8,128)S(1)} %copy.156), channel_id=1, source_target_pairs={{0,4},{4,8},{8,12},{12,16},{16,20},{20,24},{24,28},{1,5},{5,9},{9,... | collective-permute-start | bytes 245768 | tf_op jit(solution)/shard_map/while/body/eval_jaxpr/ppermute | solution.py:12
  104.9 4.7 %collective-permute-done = f32[64,5,64]{2,1,0:T(8,128)S(1)} collective-permute-done((f32[64,5,64]{2,1,0:T(8,128)S(1)}, f32[64,5,64]{2,1,0:T(8,128)S(1)}, u32[]{:S(2)}, u32[]{:S(2)}) %collective-permute-start) | collective-permute-done | bytes 81952 | tf_op jit(solution)/shard_map/while/body/eval_jaxpr/ppermute | solution.py:12
  109.6 1.3 conditional.6
  112.2 5.3 %collective-permute-start = (f32[64,5,64]{2,1,0:T(8,128)S(1)}, f32[64,5,64]{2,1,0:T(8,128)S(1)}, u32[]{:S(2)}, u32[]{:S(2)}) collective-permute-start(f32[64,5,64]{2,1,0:T(8,128)S(1)} %copy.156), channel_id=1, source_target_pairs={{0,4},{4,8},{8,12},{12,16},{16,20},{20,24},{24,28},{1,5},{5,9},{9,... | collective-permute-start | bytes 245768 | tf_op jit(solution)/shard_map/while/body/eval_jaxpr/ppermute | solution.py:12
  118.2 3.8 collective-permute-done
  122.0 1.3 conditional.6
  124.6 12.9 %collective-permute-start = (f32[64,5,64]{2,1,0:T(8,128)S(1)}, f32[64,5,64]{2,1,0:T(8,128)S(1)}, u32[]{:S(2)}, u32[]{:S(2)}) collective-permute-start(f32[64,5,64]{2,1,0:T(8,128)S(1)} %copy.156), channel_id=1, source_target_pairs={{0,4},{4,8},{8,12},{12,16},{16,20},{20,24},{24,28},{1,5},{5,9},{9,... | collective-permute-start | bytes 245768 | tf_op jit(solution)/shard_map/while/body/eval_jaxpr/ppermute | solution.py:12
  138.2 3.2 collective-permute-done
  141.3 1.3 conditional.6
  143.9 5.3 %collective-permute-start = (f32[64,5,64]{2,1,0:T(8,128)S(1)}, f32[64,5,64]{2,1,0:T(8,128)S(1)}, u32[]{:S(2)}, u32[]{:S(2)}) collective-permute-start(f32[64,5,64]{2,1,0:T(8,128)S(1)} %copy.156), channel_id=1, source_target_pairs={{0,4},{4,8},{8,12},{12,16},{16,20},{20,24},{24,28},{1,5},{5,9},{9,... | collective-permute-start | bytes 245768 | tf_op jit(solution)/shard_map/while/body/eval_jaxpr/ppermute | solution.py:12
  149.9 3.2 collective-permute-done
  153.1 1.3 conditional.6
  157.1 1.5 collective-permute-start.6
  162.5 221.7 %while.37 = (s32[]{:T(128)}, f32[64,5,64]{0,2,1:T(8,128)}, f32[1,64,5,64]{1,3,2,0:T(8,128)S(1)}, s32[]{:T(128)}, f32[1,64,5,64]{3,2,1,0:T(8,128)S(1)}, /*index=5...) while((s32[]{:T(128)}, f32[64,5,64]{0,2,1:T(8,128)}, ...), condition=%wide.region_7.9_spmd.clone, body=%wide.region_4.8_spmd.clone.sunk | while | flops 36722056 | bytes 15455306 | solution.py:145
  165.6 18.7 %collective-permute-done.1 = f32[64,5,64]{2,1,0:T(8,128)S(1)} collective-permute-done((f32[64,5,64]{2,1,0:T(8,128)S(1)}, f32[64,5,64]{2,1,0:T(8,128)S(1)}, u32[]{:S(2)}, u32[]{:S(2)}) %collective-permute-start.1) | collective-permute-done | bytes 81952 | tf_op jit(solution)/shard_map/while/body/eval_jaxpr/ppermute | solution.py:12
  184.3 1.3 conditional.7
  188.8 9.9 %collective-permute-done.1 = f32[64,5,64]{2,1,0:T(8,128)S(1)} collective-permute-done((f32[64,5,64]{2,1,0:T(8,128)S(1)}, f32[64,5,64]{2,1,0:T(8,128)S(1)}, u32[]{:S(2)}, u32[]{:S(2)}) %collective-permute-start.1) | collective-permute-done | bytes 81952 | tf_op jit(solution)/shard_map/while/body/eval_jaxpr/ppermute | solution.py:12
  198.7 1.3 conditional.7
  203.2 16.9 %collective-permute-done.1 = f32[64,5,64]{2,1,0:T(8,128)S(1)} collective-permute-done((f32[64,5,64]{2,1,0:T(8,128)S(1)}, f32[64,5,64]{2,1,0:T(8,128)S(1)}, u32[]{:S(2)}, u32[]{:S(2)}) %collective-permute-start.1) | collective-permute-done | bytes 81952 | tf_op jit(solution)/shard_map/while/body/eval_jaxpr/ppermute | solution.py:12
  220.1 1.3 conditional.7
  224.5 8.9 %collective-permute-done.1 = f32[64,5,64]{2,1,0:T(8,128)S(1)} collective-permute-done((f32[64,5,64]{2,1,0:T(8,128)S(1)}, f32[64,5,64]{2,1,0:T(8,128)S(1)}, u32[]{:S(2)}, u32[]{:S(2)}) %collective-permute-start.1) | collective-permute-done | bytes 81952 | tf_op jit(solution)/shard_map/while/body/eval_jaxpr/ppermute | solution.py:12
  233.4 1.3 conditional.7
  237.9 16.3 %collective-permute-done.1 = f32[64,5,64]{2,1,0:T(8,128)S(1)} collective-permute-done((f32[64,5,64]{2,1,0:T(8,128)S(1)}, f32[64,5,64]{2,1,0:T(8,128)S(1)}, u32[]{:S(2)}, u32[]{:S(2)}) %collective-permute-start.1) | collective-permute-done | bytes 81952 | tf_op jit(solution)/shard_map/while/body/eval_jaxpr/ppermute | solution.py:12
  254.2 1.3 conditional.7
  258.6 7.7 %collective-permute-done.1 = f32[64,5,64]{2,1,0:T(8,128)S(1)} collective-permute-done((f32[64,5,64]{2,1,0:T(8,128)S(1)}, f32[64,5,64]{2,1,0:T(8,128)S(1)}, u32[]{:S(2)}, u32[]{:S(2)}) %collective-permute-start.1) | collective-permute-done | bytes 81952 | tf_op jit(solution)/shard_map/while/body/eval_jaxpr/ppermute | solution.py:12
  266.3 1.3 conditional.7
  270.7 14.1 %collective-permute-done.1 = f32[64,5,64]{2,1,0:T(8,128)S(1)} collective-permute-done((f32[64,5,64]{2,1,0:T(8,128)S(1)}, f32[64,5,64]{2,1,0:T(8,128)S(1)}, u32[]{:S(2)}, u32[]{:S(2)}) %collective-permute-start.1) | collective-permute-done | bytes 81952 | tf_op jit(solution)/shard_map/while/body/eval_jaxpr/ppermute | solution.py:12
  284.8 1.3 conditional.7
  289.3 82.4 %collective-permute-done.1 = f32[64,5,64]{2,1,0:T(8,128)S(1)} collective-permute-done((f32[64,5,64]{2,1,0:T(8,128)S(1)}, f32[64,5,64]{2,1,0:T(8,128)S(1)}, u32[]{:S(2)}, u32[]{:S(2)}) %collective-permute-start.1) | collective-permute-done | bytes 81952 | tf_op jit(solution)/shard_map/while/body/eval_jaxpr/ppermute | solution.py:12
  371.7 11.6 %conditional.7 = (f32[1,64,5,64]{1,3,2,0:T(8,128)}, f32[64,5,64]{0,2,1:T(8,128)}) conditional(s32[]{:T(128)} %convert_element_type.71, () %tuple.118, (f32[1,64,5,64]{3,2,1,0:T(8,128)S(1)}, s32[]{:T(128)}, s32[1,64]{1,0:T(1,128)S(1)}, f32[64,5,64]{2,1,0:T(8,128)S(1)}, f32[64,64]{1,0:T(8,128)S(1)}, /*index=5*/f32[1,64,1,25]{1,3,2,0:T(8,128)S(1)}, ...), branch_computations={%region_5.6_spmd, %region_6.7_spmd} | conditional | flops 36680964 | bytes 14717496 | solution.py:135
  373.8 7.1 %multiply_reduce_fusion.1 = f32[64,320]{1,0:T(8,128)S(1)} fusion(f32[64,320]{1,0:T(8,128)S(1)} %copy.125, bf16[1,64,320,320]{3,2,1,0:T(8,128)(2,1)} %get-tuple-element.511), kind=kLoop, calls=%fused_computation.22 | loop fusion | flops 19640320 | bytes 13271040 | tf_op jit(solution)/shard_map/while/body/eval_jaxpr/cond
  381.7 1.6 copy.165
  (179 shorter events, 88.3 us)
Async XLA Ops:
  2.5 12.5 %collective-permute-start.2 = (f32[64,5,64]{2,0,1:T(8,128)S(1)}, f32[64,5,64]{2,0,1:T(8,128)S(1)}, u32[]{:S(2)}, u32[]{:S(2)}) collective-permute-start(f32[64,5,64]{2,0,1:T(8,128)S(1)} %broadcast_multiply_fusion.3), channel_id=1, source_target_pairs={{4,0},{8,4},{12,8},{16,12},{20,16},{24,20},{28,24},{5,1},{9,5},{13... | collective-permute-start | bytes 245768 | tf_op jit(solution)/shard_map/ppermute | solution.py:12
  4.0 8.9 %collective-permute-start.3 = (f32[1,1,5,64]{3,1,2,0:T(1,128)S(1)}, f32[1,1,5,64]{3,1,2,0:T(1,128)S(1)}, u32[]{:S(2)}, u32[]{:S(2)}) collective-permute-start(f32[1,1,5,64]{3,1,2,0:T(1,128)S(1)} %get-tuple-element.670), channel_id=1, source_target_pairs={{0,1},{1,2},{2,3},{4,5},{5,6},{6,7},{8,9},{9,10},{10,11},{12,13},{... | collective-permute-start | bytes 3848 | tf_op jit(solution)/shard_map/ppermute | solution.py:23
  6.4 7.6 %collective-permute-start.4 = (f32[1,1,5,64]{3,1,2,0:T(1,128)S(1)}, f32[1,1,5,64]{3,1,2,0:T(1,128)S(1)}, u32[]{:S(2)}, u32[]{:S(2)}) collective-permute-start(f32[1,1,5,64]{3,1,2,0:T(1,128)S(1)} %get-tuple-element.669), channel_id=1, source_target_pairs={{1,0},{2,1},{3,2},{5,4},{6,5},{7,6},{9,8},{10,9},{11,10},{13,12},{... | collective-permute-start | bytes 3848 | tf_op jit(solution)/shard_map/ppermute | solution.py:25
  19.6 137.3 %copy-start = (f32[4,64,64]{2,1,0:T(8,128)S(1)}, f32[4,64,64]{2,1,0:T(8,128)}, u32[]{:S(2)}) copy-start(f32[4,64,64]{2,1,0:T(8,128)} %param.22) | copy-start | bytes 196612
  20.7 9.5 %collective-permute-start = (f32[64,5,64]{2,1,0:T(8,128)S(1)}, f32[64,5,64]{2,1,0:T(8,128)S(1)}, u32[]{:S(2)}, u32[]{:S(2)}) collective-permute-start(f32[64,5,64]{2,1,0:T(8,128)S(1)} %copy.156), channel_id=1, source_target_pairs={{0,4},{4,8},{8,12},{12,16},{16,20},{20,24},{24,28},{1,5},{5,9},{9,... | collective-permute-start | bytes 245768 | tf_op jit(solution)/shard_map/while/body/eval_jaxpr/ppermute | solution.py:12
  43.9 6.4 %collective-permute-start = (f32[64,5,64]{2,1,0:T(8,128)S(1)}, f32[64,5,64]{2,1,0:T(8,128)S(1)}, u32[]{:S(2)}, u32[]{:S(2)}) collective-permute-start(f32[64,5,64]{2,1,0:T(8,128)S(1)} %copy.156), channel_id=1, source_target_pairs={{0,4},{4,8},{8,12},{12,16},{16,20},{20,24},{24,28},{1,5},{5,9},{9,... | collective-permute-start | bytes 245768 | tf_op jit(solution)/shard_map/while/body/eval_jaxpr/ppermute | solution.py:12
  52.9 21.9 %collective-permute-start = (f32[64,5,64]{2,1,0:T(8,128)S(1)}, f32[64,5,64]{2,1,0:T(8,128)S(1)}, u32[]{:S(2)}, u32[]{:S(2)}) collective-permute-start(f32[64,5,64]{2,1,0:T(8,128)S(1)} %copy.156), channel_id=1, source_target_pairs={{0,4},{4,8},{8,12},{12,16},{16,20},{20,24},{24,28},{1,5},{5,9},{9,... | collective-permute-start | bytes 245768 | tf_op jit(solution)/shard_map/while/body/eval_jaxpr/ppermute | solution.py:12
  77.4 10.2 %collective-permute-start = (f32[64,5,64]{2,1,0:T(8,128)S(1)}, f32[64,5,64]{2,1,0:T(8,128)S(1)}, u32[]{:S(2)}, u32[]{:S(2)}) collective-permute-start(f32[64,5,64]{2,1,0:T(8,128)S(1)} %copy.156), channel_id=1, source_target_pairs={{0,4},{4,8},{8,12},{12,16},{16,20},{20,24},{24,28},{1,5},{5,9},{9,... | collective-permute-start | bytes 245768 | tf_op jit(solution)/shard_map/while/body/eval_jaxpr/ppermute | solution.py:12
  90.3 19.4 %collective-permute-start = (f32[64,5,64]{2,1,0:T(8,128)S(1)}, f32[64,5,64]{2,1,0:T(8,128)S(1)}, u32[]{:S(2)}, u32[]{:S(2)}) collective-permute-start(f32[64,5,64]{2,1,0:T(8,128)S(1)} %copy.156), channel_id=1, source_target_pairs={{0,4},{4,8},{8,12},{12,16},{16,20},{20,24},{24,28},{1,5},{5,9},{9,... | collective-permute-start | bytes 245768 | tf_op jit(solution)/shard_map/while/body/eval_jaxpr/ppermute | solution.py:12
  112.2 9.8 %collective-permute-start = (f32[64,5,64]{2,1,0:T(8,128)S(1)}, f32[64,5,64]{2,1,0:T(8,128)S(1)}, u32[]{:S(2)}, u32[]{:S(2)}) collective-permute-start(f32[64,5,64]{2,1,0:T(8,128)S(1)} %copy.156), channel_id=1, source_target_pairs={{0,4},{4,8},{8,12},{12,16},{16,20},{20,24},{24,28},{1,5},{5,9},{9,... | collective-permute-start | bytes 245768 | tf_op jit(solution)/shard_map/while/body/eval_jaxpr/ppermute | solution.py:12
  124.6 16.8 %collective-permute-start = (f32[64,5,64]{2,1,0:T(8,128)S(1)}, f32[64,5,64]{2,1,0:T(8,128)S(1)}, u32[]{:S(2)}, u32[]{:S(2)}) collective-permute-start(f32[64,5,64]{2,1,0:T(8,128)S(1)} %copy.156), channel_id=1, source_target_pairs={{0,4},{4,8},{8,12},{12,16},{16,20},{20,24},{24,28},{1,5},{5,9},{9,... | collective-permute-start | bytes 245768 | tf_op jit(solution)/shard_map/while/body/eval_jaxpr/ppermute | solution.py:12
  143.9 9.2 %collective-permute-start = (f32[64,5,64]{2,1,0:T(8,128)S(1)}, f32[64,5,64]{2,1,0:T(8,128)S(1)}, u32[]{:S(2)}, u32[]{:S(2)}) collective-permute-start(f32[64,5,64]{2,1,0:T(8,128)S(1)} %copy.156), channel_id=1, source_target_pairs={{0,4},{4,8},{8,12},{12,16},{16,20},{20,24},{24,28},{1,5},{5,9},{9,... | collective-permute-start | bytes 245768 | tf_op jit(solution)/shard_map/while/body/eval_jaxpr/ppermute | solution.py:12
  154.8 5.3 %collective-permute-start.5 = (f32[1,1,5,64]{3,1,2,0:T(1,128)S(1)}, f32[1,1,5,64]{3,1,2,0:T(1,128)S(1)}, u32[]{:S(2)}, u32[]{:S(2)}) collective-permute-start(f32[1,1,5,64]{3,1,2,0:T(1,128)S(1)} %get-tuple-element.668), channel_id=1, source_target_pairs={{0,1},{1,2},{2,3},{4,5},{5,6},{6,7},{8,9},{9,10},{10,11},{12,13},{... | collective-permute-start | bytes 3848 | tf_op jit(solution)/shard_map/ppermute | solution.py:23
  157.1 3.8 collective-permute-start.6
  163.6 20.7 %collective-permute-start.1 = (f32[64,5,64]{2,1,0:T(8,128)S(1)}, f32[64,5,64]{2,1,0:T(8,128)S(1)}, u32[]{:S(2)}, u32[]{:S(2)}) collective-permute-start(f32[64,5,64]{2,1,0:T(8,128)S(1)} %copy.157), channel_id=1, source_target_pairs={{4,0},{8,4},{12,8},{16,12},{20,16},{24,20},{28,24},{5,1},{9,5},{13... | collective-permute-start | bytes 245768 | tf_op jit(solution)/shard_map/while/body/eval_jaxpr/ppermute | solution.py:12
  186.8 11.9 %collective-permute-start.1 = (f32[64,5,64]{2,1,0:T(8,128)S(1)}, f32[64,5,64]{2,1,0:T(8,128)S(1)}, u32[]{:S(2)}, u32[]{:S(2)}) collective-permute-start(f32[64,5,64]{2,1,0:T(8,128)S(1)} %copy.157), channel_id=1, source_target_pairs={{4,0},{8,4},{12,8},{16,12},{20,16},{24,20},{28,24},{5,1},{9,5},{13... | collective-permute-start | bytes 245768 | tf_op jit(solution)/shard_map/while/body/eval_jaxpr/ppermute | solution.py:12
  201.2 18.9 %collective-permute-start.1 = (f32[64,5,64]{2,1,0:T(8,128)S(1)}, f32[64,5,64]{2,1,0:T(8,128)S(1)}, u32[]{:S(2)}, u32[]{:S(2)}) collective-permute-start(f32[64,5,64]{2,1,0:T(8,128)S(1)} %copy.157), channel_id=1, source_target_pairs={{4,0},{8,4},{12,8},{16,12},{20,16},{24,20},{28,24},{5,1},{9,5},{13... | collective-permute-start | bytes 245768 | tf_op jit(solution)/shard_map/while/body/eval_jaxpr/ppermute | solution.py:12
  222.6 10.8 %collective-permute-start.1 = (f32[64,5,64]{2,1,0:T(8,128)S(1)}, f32[64,5,64]{2,1,0:T(8,128)S(1)}, u32[]{:S(2)}, u32[]{:S(2)}) collective-permute-start(f32[64,5,64]{2,1,0:T(8,128)S(1)} %copy.157), channel_id=1, source_target_pairs={{4,0},{8,4},{12,8},{16,12},{20,16},{24,20},{28,24},{5,1},{9,5},{13... | collective-permute-start | bytes 245768 | tf_op jit(solution)/shard_map/while/body/eval_jaxpr/ppermute | solution.py:12
  235.9 18.3 %collective-permute-start.1 = (f32[64,5,64]{2,1,0:T(8,128)S(1)}, f32[64,5,64]{2,1,0:T(8,128)S(1)}, u32[]{:S(2)}, u32[]{:S(2)}) collective-permute-start(f32[64,5,64]{2,1,0:T(8,128)S(1)} %copy.157), channel_id=1, source_target_pairs={{4,0},{8,4},{12,8},{16,12},{20,16},{24,20},{28,24},{5,1},{9,5},{13... | collective-permute-start | bytes 245768 | tf_op jit(solution)/shard_map/while/body/eval_jaxpr/ppermute | solution.py:12
  256.6 9.6 %collective-permute-start.1 = (f32[64,5,64]{2,1,0:T(8,128)S(1)}, f32[64,5,64]{2,1,0:T(8,128)S(1)}, u32[]{:S(2)}, u32[]{:S(2)}) collective-permute-start(f32[64,5,64]{2,1,0:T(8,128)S(1)} %copy.157), channel_id=1, source_target_pairs={{4,0},{8,4},{12,8},{16,12},{20,16},{24,20},{28,24},{5,1},{9,5},{13... | collective-permute-start | bytes 245768 | tf_op jit(solution)/shard_map/while/body/eval_jaxpr/ppermute | solution.py:12
  268.8 16.1 %collective-permute-start.1 = (f32[64,5,64]{2,1,0:T(8,128)S(1)}, f32[64,5,64]{2,1,0:T(8,128)S(1)}, u32[]{:S(2)}, u32[]{:S(2)}) collective-permute-start(f32[64,5,64]{2,1,0:T(8,128)S(1)} %copy.157), channel_id=1, source_target_pairs={{4,0},{8,4},{12,8},{16,12},{20,16},{24,20},{28,24},{5,1},{9,5},{13... | collective-permute-start | bytes 245768 | tf_op jit(solution)/shard_map/while/body/eval_jaxpr/ppermute | solution.py:12
  287.3 84.4 %collective-permute-start.1 = (f32[64,5,64]{2,1,0:T(8,128)S(1)}, f32[64,5,64]{2,1,0:T(8,128)S(1)}, u32[]{:S(2)}, u32[]{:S(2)}) collective-permute-start(f32[64,5,64]{2,1,0:T(8,128)S(1)} %copy.157), channel_id=1, source_target_pairs={{4,0},{8,4},{12,8},{16,12},{20,16},{24,20},{28,24},{5,1},{9,5},{13... | collective-permute-start | bytes 245768 | tf_op jit(solution)/shard_map/while/body/eval_jaxpr/ppermute | solution.py:12
where the time goes:
time: 387 us; the launch traced here: 385 us
  waiting for transfers between devices  209 us (54%)
  starting transfers between devices  81.6 us (21%)
  local copies, waits for them, and re-layouts  50.6 us (13%)
  other arithmetic  31.4 us (8%)
  matrix products  9.56 us (2%)
    ppermute x17, waiting for transfers between devices, passed_along(): return lax.ppermute(block, axis, route)  209 us
    ppermute x17, starting transfers between devices, passed_along(): return lax.ppermute(block, axis, route)  75.2 us
    another operation x38, local copies, waits for them, and re-layouts  20.8 us
    while x16, local copies, waits for them, and re-layouts  17.1 us
    cond x4, other arithmetic  14.3 us
    convert_element_type x17, other arithmetic, per_device(): live = (slot_index[None, :] < live_counts).astype(jnp.float32)  10.4 us
  transfers between devices with their start and end apart: 21, of which 16 were waited for; matrix products, arithmetic and copies ran while one was open for 5% of the time, Pallas kernels for 0%

commit v1 on v0

v1 whole, which is shorter than its diff:
```python
import functools

import jax
import jax.numpy as jnp
from jax import lax
from jax.experimental import pallas as pl
from jax.experimental.pallas import tpu as pltpu
from jax.sharding import PartitionSpec as P

NVAR = 5
GROUP = 8
MESH = pl.DeviceIdType.MESH
CONTRACT_LAST = (((1,), (1,)), ((), ()))


def sweep_kernel(
    nf, nc,
    rhs, old, ainv, jac, lift, up, down, cnt,
    half_out, full_out,
    a_vm, jx, lt, oldp, halfp, down_in, halo, fwd_in, bwd_in, fix_f, fix_b, rel,
    a_sem, old_send, old_recv, halo_send, halo_recv, fwd_send, fwd_recv, bwd_send, bwd_recv,
):
    elems, unk = rhs.shape[1], rhs.shape[2]
    nb = unk // NVAR
    wide = -(-unk // 128) * 128
    groups = elems // GROUP
    f = lax.axis_index("flow")
    c = lax.axis_index("cross")
    has_up, has_down = f > 0, f < nf - 1
    has_left, has_right = c > 0, c < nc - 1
    up_dev, down_dev = {"flow": f - 1}, {"flow": f + 1}
    left_dev, right_dev = {"cross": c - 1}, {"cross": c + 1}
    neighbours = ((has_up, up_dev), (has_down, down_dev), (has_left, left_dev), (has_right, right_dev))

    def rows(g):
        return pl.ds(pl.multiple_of(g * GROUP, GROUP), GROUP)

    def padded_rows(g):
        return pl.ds(pl.multiple_of(g * GROUP + GROUP, GROUP), GROUP)

    def a_copy(g):
        return pltpu.make_async_copy(ainv.at[0, rows(g)], a_vm.at[rows(g)], a_sem.at[g])

    def remote(src, dst, ssem, rsem, dev):
        return pltpu.make_async_remote_copy(
            src_ref=src, dst_ref=dst, send_sem=ssem, recv_sem=rsem,
            device_id=dev, device_id_type=MESH,
        )

    def old_copy():
        return remote(oldp.at[pl.ds(GROUP, elems)], down_in, old_send, old_recv, up_dev)

    def halo_copy(buf, which, slot, dev):
        start = elems if which == 0 else GROUP
        return remote(buf.at[pl.ds(start, GROUP)], halo.at[slot], halo_send.at[slot], halo_recv.at[slot], dev)

    def fwd_copy(g):
        return remote(halfp.at[padded_rows(g)], fwd_in.at[g], fwd_send.at[g], fwd_recv.at[g], down_dev)

    def bwd_copy(g):
        return remote(full_out.at[0, rows(g)], bwd_in.at[g], bwd_send.at[g], bwd_recv.at[g], up_dev)

    for g in range(groups):
        a_copy(g).start()

    barrier = pltpu.get_barrier_semaphore()
    for there, dev in neighbours:
        @pl.when(there)
        def _(dev=dev):
            pl.semaphore_signal(barrier, inc=1, device_id=dev, device_id_type=MESH)

    count = cnt[0, 0]
    slot = lax.broadcasted_iota(jnp.int32, (elems, unk), 0)
    oldp[pl.ds(GROUP, elems)] = jnp.where(slot < count, old[0], 0.0)

    pl.semaphore_wait(barrier, sum(there.astype(jnp.int32) for there, _ in neighbours))

    @pl.when(has_up)
    def _():
        old_copy().start()

    @pl.when(has_right)
    def _():
        halo_copy(oldp, 0, 0, right_dev).start()

    @pl.when(has_left)
    def _():
        halo_copy(oldp, 1, 1, left_dev).start()

    edge = jnp.zeros((GROUP, unk), jnp.float32)

    @pl.when(jnp.logical_not(has_up))
    def _():
        fwd_in[...] = jnp.zeros_like(fwd_in)

    @pl.when(jnp.logical_not(has_down))
    def _():
        down_in[...] = jnp.zeros_like(down_in)
        bwd_in[...] = jnp.zeros_like(bwd_in)

    @pl.when(jnp.logical_not(has_left))
    def _():
        halo[0] = edge
        halo[2] = edge

    @pl.when(jnp.logical_not(has_right))
    def _():
        halo[1] = edge
        halo[3] = edge

    square = (elems, elems)
    diagonal = lax.broadcasted_iota(jnp.int32, square, 0) == lax.broadcasted_iota(jnp.int32, square, 1)
    for i, index in enumerate((up, down)):
        local = (index[...] % GROUP).astype(jnp.float32)
        column = jnp.sum(jnp.where(diagonal, jnp.broadcast_to(local, square), 0.0), axis=1, keepdims=True)
        rel[i] = jnp.broadcast_to(column, (elems, 128))

    n2 = NVAR * NVAR
    entry = lax.broadcasted_iota(jnp.int32, (n2, NVAR * wide), 0)
    place = lax.broadcasted_iota(jnp.int32, (n2, NVAR * wide), 1)
    wanted = ((place % wide) // nb) * NVAR + place // wide
    spread_one = jnp.where(entry == wanted, 1.0, 0.0).astype(jnp.bfloat16)
    for d in range(4):
        block = lift[d].astype(jnp.bfloat16)
        lt[d] = jnp.concatenate([block] * NVAR, axis=0)
        values = jac[0, :, d, :]
        high = values.astype(jnp.bfloat16)
        low = (values - high.astype(jnp.float32)).astype(jnp.bfloat16)
        jx[d] = jnp.dot(high, spread_one, preferred_element_type=jnp.float32) + jnp.dot(
            low, spread_one, preferred_element_type=jnp.float32
        )

    def permuted(x, which, g):
        column = rel[which, rows(g)][:, 0:1]
        out = jnp.zeros_like(x)
        for k in range(GROUP):
            out = jnp.where(column == float(k), x[k : k + 1], out)
        return out

    def couple(x, d, where):
        n = x.shape[0]
        stacked = jnp.concatenate([x[:, v * nb : (v + 1) * nb] for v in range(NVAR)], axis=0)
        spread = lax.dot_general(
            stacked.astype(jnp.bfloat16), lt[d], CONTRACT_LAST, preferred_element_type=jnp.float32
        )
        total = None
        for v in range(NVAR):
            term = jx[d, where, v * wide : v * wide + unk] * spread[v * n : (v + 1) * n]
            total = term if total is None else total + term
        return total

    def solve(resid, g):
        flat = resid.astype(jnp.bfloat16)
        row = lax.broadcasted_iota(jnp.int32, (GROUP, unk), 0)
        out = jnp.zeros((GROUP, unk), jnp.float32)
        for k in range(GROUP):
            product = lax.dot_general(
                flat, a_vm[g * GROUP + k], CONTRACT_LAST, preferred_element_type=jnp.float32
            )
            out = jnp.where(row == k, product, out)
        return jnp.where(row + g * GROUP < count, out, 0.0)

    @pl.when(has_left)
    def _():
        halo_copy(oldp, 0, 0, right_dev).wait_recv()

    @pl.when(has_right)
    def _():
        halo_copy(oldp, 1, 1, left_dev).wait_recv()

    oldp[pl.ds(0, GROUP)] = halo[0]
    oldp[pl.ds(elems + GROUP, GROUP)] = halo[1]

    whole = pl.ds(0, elems)
    fix_f[...] = (
        rhs[0]
        - couple(oldp[pl.ds(GROUP - 1, elems)], 2, whole)
        - couple(oldp[pl.ds(GROUP + 1, elems)], 3, whole)
    )

    @pl.when(has_down)
    def _():
        old_copy().wait_recv()

    def arrange(g, carry):
        oldp[rows(g)] = permuted(down_in[rows(g)], 1, g)
        return carry

    @pl.when(has_up)
    def _():
        old_copy().wait_send()

    @pl.when(has_right)
    def _():
        halo_copy(oldp, 0, 0, right_dev).wait_send()

    @pl.when(has_left)
    def _():
        halo_copy(oldp, 1, 1, left_dev).wait_send()

    lax.fori_loop(0, groups, arrange, 0)
    fix_f[...] = fix_f[...] - couple(oldp[pl.ds(0, elems)], 1, whole)

    def forward(g, carry):
        a_copy(g).wait()

        @pl.when(has_up)
        def _():
            fwd_copy(g).wait_recv()

        coupled = couple(permuted(fwd_in[g], 0, g), 0, rows(g))
        fix_b[rows(g)] = rhs[0, rows(g)] - coupled
        solved = solve(fix_f[rows(g)] - coupled, g)
        halfp[padded_rows(g)] = solved

        @pl.when(has_down)
        def _():
            fwd_copy(g).start()

        half_out[0, rows(g)] = solved

        @pl.when(jnp.logical_and(g == 0, has_left))
        def _():
            halo_copy(halfp, 1, 3, left_dev).start()

        return carry

    lax.fori_loop(0, groups, forward, 0)

    @pl.when(has_right)
    def _():
        halo_copy(halfp, 0, 2, right_dev).start()
        halo_copy(halfp, 1, 3, left_dev).wait_recv()

    @pl.when(has_left)
    def _():
        halo_copy(halfp, 0, 2, right_dev).wait_recv()

    halfp[pl.ds(0, GROUP)] = halo[2]
    halfp[pl.ds(elems + GROUP, GROUP)] = halo[3]
    fix_b[...] = (
        fix_b[...]
        - couple(halfp[pl.ds(GROUP - 1, elems)], 2, whole)
        - couple(halfp[pl.ds(GROUP + 1, elems)], 3, whole)
    )

    def backward(i, carry):
        g = groups - 1 - i

        @pl.when(has_down)
        def _():
            bwd_copy(g).wait_recv()

        coupled = couple(permuted(bwd_in[g], 1, g), 1, rows(g))
        full_out[0, rows(g)] = solve(fix_b[rows(g)] - coupled, g)

        @pl.when(has_up)
        def _():
            bwd_copy(g).start()

        return carry

    lax.fori_loop(0, groups, backward, 0)

    def drain(g, carry):
        @pl.when(has_down)
        def _():
            fwd_copy(g).wait_send()

        @pl.when(has_up)
        def _():
            bwd_copy(g).wait_send()

        return carry

    lax.fori_loop(0, groups, drain, 0)

    @pl.when(has_right)
    def _():
        halo_copy(halfp, 0, 2, right_dev).wait_send()

    @pl.when(has_left)
    def _():
        halo_copy(halfp, 1, 3, left_dev).wait_send()


def per_device(
    right_side, old_state, block_inverse, flux_jacobian, face_lift, upstream, downstream, live_counts
):
    layers, elems, unk = right_side.shape
    assert layers == 1 and elems % GROUP == 0
    nf, nc = lax.axis_size("flow"), lax.axis_size("cross")
    nb = unk // NVAR
    wide = -(-unk // 128) * 128
    groups = elems // GROUP
    vmem = pl.BlockSpec(memory_space=pltpu.VMEM)
    f32 = jnp.float32
    dma = pltpu.SemaphoreType.DMA
    return pl.pallas_call(
        functools.partial(sweep_kernel, nf, nc),
        out_shape=(jax.ShapeDtypeStruct(right_side.shape, f32),) * 2,
        in_specs=[
            vmem, vmem, pl.BlockSpec(memory_space=pl.ANY), vmem, vmem, vmem, vmem,
            pl.BlockSpec(memory_space=pltpu.SMEM),
        ],
        out_specs=(vmem, vmem),
        scratch_shapes=[
            pltpu.VMEM((elems, unk, unk), jnp.bfloat16),
            pltpu.VMEM((4, elems, NVAR * wide), f32),
            pltpu.VMEM((4, unk, nb), jnp.bfloat16),
            pltpu.VMEM((elems + 2 * GROUP, unk), f32),
            pltpu.VMEM((elems + 2 * GROUP, unk), f32),
            pltpu.VMEM((elems, unk), f32),
            pltpu.VMEM((4, GROUP, unk), f32),
            pltpu.VMEM((groups, GROUP, unk), f32),
            pltpu.VMEM((groups, GROUP, unk), f32),
            pltpu.VMEM((elems, unk), f32),
            pltpu.VMEM((elems, unk), f32),
            pltpu.VMEM((2, elems, 128), f32),
            dma((groups,)), dma, dma, dma((4,)), dma((4,)),
            dma((groups,)), dma((groups,)), dma((groups,)), dma((groups,)),
        ],
        compiler_params=pltpu.CompilerParams(
            collective_id=0, has_side_effects=True, vmem_limit_bytes=40 * 1024 * 1024
        ),
        cost_estimate=pl.CostEstimate(
            flops=4 * elems * unk * unk, bytes_accessed=2 * elems * unk * unk, transcendentals=0
        ),
        name="sweep",
    )(right_side, old_state, block_inverse, flux_jacobian, face_lift, upstream, downstream, live_counts)


def solution(mesh):
    in_specs = (
        P("flow", "cross", None),
        P("flow", "cross", None),
        P("flow", "cross", None, None),
        P("flow", "cross", None, None),
        P(),
        P("flow", "cross"),
        P("flow", "cross"),
        P("flow", "cross"),
    )
    out_specs = (P("flow", "cross", None), P("flow", "cross", None))
    return jax.shard_map(
        per_device, mesh=mesh, in_specs=in_specs, out_specs=out_specs, check_vma=False
    )
```

time: 387 us -> 84.8 us (0.22)
  waiting for transfers between devices: 209 us -> 0 us
  starting transfers between devices: 81.6 us -> 0 us
  Pallas kernels: 0 us -> 77 us
  local copies, waits for them, and re-layouts: 50.6 us -> 6.2 us
  other arithmetic: 31.4 us -> 0 us
  matrix products: 9.56 us -> 0 us
    ppermute x21 -> x0, waiting for transfers between devices: 209 us -> none  [the longest x17 209 us: passed_along(): return lax.ppermute(block, axis, route)]
    ppermute x21 -> x0, starting transfers between devices: 81.6 us -> none  [the longest x17 75.2 us: passed_along(): return lax.ppermute(block, axis, route)]
    pallas_call x0 -> x1, Pallas kernels: none -> 77 us  [per_device(): pl.pallas_call(functools.partial(sweep_kernel, nf, nc), out_shape=(jax.Sh...]
    another operation x43 -> x0, local copies, waits for them, and re-layouts: 21.3 us -> none
    while x17 -> x0, local copies, waits for them, and re-layouts: 17.2 us -> none
    cond x4 -> x0, other arithmetic: 14.3 us -> none
    convert_element_type x17 -> x0, other arithmetic: 10.4 us -> none  [per_device(): live = (slot_index[None, :] < live_counts).astype(jnp.float32)]
    dot_general x16 -> x0, matrix products: 9.56 us -> none  [the longest x8 5 us: couple(): jnp.einsum('...uv,...vb->...ub', mixing, spread, precision=HIGHEST_PRECIS...]
  transfers between devices with their start and end apart: 21 -> 0, of which waited for: 16 -> 0; matrix products, arithmetic and copies ran while one was open for 5% -> 0% of each run, Pallas kernels for 0% -> 0%
where the time goes in v1:
time: 84.8 us; the launch traced here: 84.5 us
  Pallas kernels  77 us (91%)
  local copies, waits for them, and re-layouts  6.2 us (7%)
  between operations  1.3 us (2%)
    pallas_call x1, Pallas kernels, per_device(): pl.pallas_call(functools.partial(sweep_kernel, nf, nc), out_shape=(jax.Sh...  77 us
    unnamed x13, local copies, waits for them, and re-layouts  6.2 us

profile of v1, /device:TPU:0, one launch (start us, length us, event | category | flops | bytes accessed | tf_op | source)
XLA Modules:
  0.0 84.5 jit_solution(3637336135485389130)
XLA Ops:
  1.3 0.9 %copy.10.jac = f32[1,64,4,25]{3,2,1,0:T(4,128)S(1)} copy(f32[1,64,4,25]{1,2,3,0:T(4,128)} %param.11) | data formatting | bytes 51200 | tf_op args[3]
  2.2 0.0 copy-start
  2.2 0.9 %copy-done = f32[4,64,64]{2,1,0:T(8,128)S(1)} copy-done((f32[4,64,64]{2,1,0:T(8,128)S(1)}, f32[4,64,64]{2,1,0:T(8,128)}, u32[]{:S(2)}) %copy-start) | copy-done | bytes 65560
  3.1 0.0 copy-start.1
  3.1 0.9 %copy-done.1 = f32[1,64,320]{2,1,0:T(8,128)S(1)} copy-done((f32[1,64,320]{2,1,0:T(8,128)S(1)}, f32[1,64,320]{2,1,0:T(8,128)}, u32[]{:S(2)}) %copy-start.1) | copy-done | bytes 81944
  4.0 0.0 copy-start.2
  4.0 0.9 %copy-done.2 = f32[1,64,320]{2,1,0:T(8,128)S(1)} copy-done((f32[1,64,320]{2,1,0:T(8,128)S(1)}, f32[1,64,320]{2,1,0:T(8,128)}, u32[]{:S(2)}) %copy-start.2) | copy-done | bytes 81944
  4.9 0.0 copy-start.3
  4.9 0.7 copy-done.3
  5.5 0.0 copy-start.4
  5.6 0.7 copy-done.4
  6.2 77.0 %sweep.1 = (f32[1,64,320]{2,1,0:T(8,128)S(1)}, f32[1,64,320]{2,1,0:T(8,128)S(1)}) custom-call(f32[1,64,320]{2,1,0:T(8,128)S(1)} %copy-done.1, f32[1,64,320]{2,1,0:T(8,128)S(1)} %copy-done.2, bf16[1,64,320,320]{3,2,1,0:T(8,128)(2,1)} %ainv.1, f32[1,64,4,25]{3,2,1,0:T(4,128)S(1)} %copy.10.jac, f32[4,64,64]{2,1,0:T(8,128)S(1)} %copy-done, ...), custom_call_target="tpu_custom_call" | custom-call | flops 26214400 | bytes 13107200 | tf_op jit(solution)/shard_map/sweep/pallas_call | solution.py:299
  83.2 0.6 copy.14
  83.9 0.6 copy.15
Async XLA Ops:
  2.2 0.9 %copy-start = (f32[4,64,64]{2,1,0:T(8,128)S(1)}, f32[4,64,64]{2,1,0:T(8,128)}, u32[]{:S(2)}) copy-start(f32[4,64,64]{2,1,0:T(8,128)} %lift.1) | copy-start | bytes 196612
  3.1 0.9 %copy-start.1 = (f32[1,64,320]{2,1,0:T(8,128)S(1)}, f32[1,64,320]{2,1,0:T(8,128)}, u32[]{:S(2)}) copy-start(f32[1,64,320]{2,1,0:T(8,128)} %rhs.1) | copy-start | bytes 245764
  4.0 0.9 %copy-start.2 = (f32[1,64,320]{2,1,0:T(8,128)S(1)}, f32[1,64,320]{2,1,0:T(8,128)}, u32[]{:S(2)}) copy-start(f32[1,64,320]{2,1,0:T(8,128)} %old.1) | copy-start | bytes 245764
  4.9 0.7 copy-start.3
  5.5 0.7 copy-start.4

commit v2 on v1

--- a/solution.py
+++ b/solution.py
@@ -9,18 +9,23 @@
 
 NVAR = 5
 GROUP = 8
+BLOCK = 4
+VMEM_BYTES = 64 * 1024 * 1024
 MESH = pl.DeviceIdType.MESH
 CONTRACT_LAST = (((1,), (1,)), ((), ()))
+CONTRACT_FIRST = (((0,), (0,)), ((), ()))
 
 
 def sweep_kernel(
     nf, nc,
-    rhs, old, ainv, jac, lift, up, down, cnt,
+    rhs_hbm, old_hbm, ainv, jac_hbm, lift_hbm, up_hbm, down_hbm, cnt_hbm,
     half_out, full_out,
-    a_vm, jx, lt, oldp, halfp, down_in, halo, fwd_in, bwd_in, fix_f, fix_b, rel,
-    a_sem, old_send, old_recv, halo_send, halo_recv, fwd_send, fwd_recv, bwd_send, bwd_recv,
+    rhs, old, jac, lift, up, down, cnt,
+    a_vm, jx, lt, oldp, halfp, down_in, halo, fwd_in, bwd_in, fwd_snd, bwd_snd, fix_f, fix_b, rel,
+    in_sem, a_sem, old_send, old_recv, halo_send, halo_recv, fwd_send, fwd_recv, bwd_send, bwd_recv,
 ):
     elems, unk = rhs.shape[1], rhs.shape[2]
+    halves = GROUP // BLOCK
     nb = unk // NVAR
     wide = -(-unk // 128) * 128
     groups = elems // GROUP
@@ -55,11 +60,18 @@
         return remote(buf.at[pl.ds(start, GROUP)], halo.at[slot], halo_send.at[slot], halo_recv.at[slot], dev)
 
     def fwd_copy(g):
-        return remote(halfp.at[padded_rows(g)], fwd_in.at[g], fwd_send.at[g], fwd_recv.at[g], down_dev)
+        return remote(fwd_snd.at[g], fwd_in.at[g], fwd_send.at[g], fwd_recv.at[g], down_dev)
 
     def bwd_copy(g):
-        return remote(full_out.at[0, rows(g)], bwd_in.at[g], bwd_send.at[g], bwd_recv.at[g], up_dev)
-
+        return remote(bwd_snd.at[g], bwd_in.at[g], bwd_send.at[g], bwd_recv.at[g], up_dev)
+
+    sources = (old_hbm, cnt_hbm, jac_hbm, lift_hbm, up_hbm, down_hbm, rhs_hbm)
+    fetches = [
+        pltpu.make_async_copy(src, dst, in_sem.at[i])
+        for i, (src, dst) in enumerate(zip(sources, (old, cnt, jac, lift, up, down, rhs)))
+    ]
+    for fetch in fetches:
+        fetch.start()
     for g in range(groups):
         a_copy(g).start()
 
@@ -69,7 +81,9 @@
         def _(dev=dev):
             pl.semaphore_signal(barrier, inc=1, device_id=dev, device_id_type=MESH)
 
-    count = cnt[0, 0]
+    fetches[0].wait()
+    fetches[1].wait()
+    count = cnt[...]
     slot = lax.broadcasted_iota(jnp.int32, (elems, unk), 0)
     oldp[pl.ds(GROUP, elems)] = jnp.where(slot < count, old[0], 0.0)
 
@@ -107,11 +121,14 @@
     def _():
         halo[1] = edge
         halo[3] = edge
+
+    for fetch in fetches[2:]:
+        fetch.wait()
 
     square = (elems, elems)
     diagonal = lax.broadcasted_iota(jnp.int32, square, 0) == lax.broadcasted_iota(jnp.int32, square, 1)
     for i, index in enumerate((up, down)):
-        local = (index[...] % GROUP).astype(jnp.float32)
+        local = (index[...] % BLOCK).astype(jnp.float32)
         column = jnp.sum(jnp.where(diagonal, jnp.broadcast_to(local, square), 0.0), axis=1, keepdims=True)
         rel[i] = jnp.broadcast_to(column, (elems, 128))
 
@@ -123,17 +140,19 @@
     for d in range(4):
         block = lift[d].astype(jnp.bfloat16)
         lt[d] = jnp.concatenate([block] * NVAR, axis=0)
-        values = jac[0, :, d, :]
+        values = jac[:, d, :]
         high = values.astype(jnp.bfloat16)
         low = (values - high.astype(jnp.float32)).astype(jnp.bfloat16)
-        jx[d] = jnp.dot(high, spread_one, preferred_element_type=jnp.float32) + jnp.dot(
-            low, spread_one, preferred_element_type=jnp.float32
-        )
+        jx[d] = lax.dot_general(
+            high, spread_one, CONTRACT_FIRST, preferred_element_type=jnp.float32
+        ) + lax.dot_general(low, spread_one, CONTRACT_FIRST, preferred_element_type=jnp.float32)
+
+    row = lax.broadcasted_iota(jnp.int32, (GROUP, unk), 0)
 
     def permuted(x, which, g):
         column = rel[which, rows(g)][:, 0:1]
-        out = jnp.zeros_like(x)
-        for k in range(GROUP):
+        out = jnp.broadcast_to(x[0:1], (GROUP, unk))
+        for k in range(1, BLOCK):
             out = jnp.where(column == float(k), x[k : k + 1], out)
         return out
 
@@ -149,11 +168,10 @@
             total = term if total is None else total + term
         return total
 
-    def solve(resid, g):
+    def solve(resid, g, h):
         flat = resid.astype(jnp.bfloat16)
-        row = lax.broadcasted_iota(jnp.int32, (GROUP, unk), 0)
         out = jnp.zeros((GROUP, unk), jnp.float32)
-        for k in range(GROUP):
+        for k in range(h * BLOCK, (h + 1) * BLOCK):
             product = lax.dot_general(
                 flat, a_vm[g * GROUP + k], CONTRACT_LAST, preferred_element_type=jnp.float32
             )
@@ -183,7 +201,8 @@
         old_copy().wait_recv()
 
     def arrange(g, carry):
-        oldp[rows(g)] = permuted(down_in[rows(g)], 1, g)
+        x = down_in[rows(g)]
+        oldp[rows(g)] = jnp.where(row < BLOCK, permuted(x[:BLOCK], 1, g), permuted(x[BLOCK:], 1, g))
         return carry
 
     @pl.when(has_up)
@@ -204,20 +223,29 @@
     def forward(g, carry):
         a_copy(g).wait()
 
-        @pl.when(has_up)
-        def _():
-            fwd_copy(g).wait_recv()
-
-        coupled = couple(permuted(fwd_in[g], 0, g), 0, rows(g))
-        fix_b[rows(g)] = rhs[0, rows(g)] - coupled
-        solved = solve(fix_f[rows(g)] - coupled, g)
-        halfp[padded_rows(g)] = solved
-
-        @pl.when(has_down)
-        def _():
-            fwd_copy(g).start()
-
-        half_out[0, rows(g)] = solved
+        fixed = fix_f[rows(g)]
+        coupling = jnp.zeros((GROUP, unk), jnp.float32)
+        result = jnp.zeros((GROUP, unk), jnp.float32)
+        for h in range(halves):
+            j = g * halves + h
+
+            @pl.when(has_up)
+            def _():
+                fwd_copy(j).wait_recv()
+
+            coupled = couple(permuted(fwd_in[j], 0, g), 0, rows(g))
+            solved = solve(fixed - coupled, g, h)
+            fwd_snd[j] = solved[h * BLOCK : (h + 1) * BLOCK]
+
+            @pl.when(has_down)
+            def _():
+                fwd_copy(j).start()
+
+            coupling = jnp.where(row // BLOCK == h, coupled, coupling)
+            result = result + solved
+        fix_b[rows(g)] = rhs[0, rows(g)] - coupling
+        halfp[padded_rows(g)] = result
+        half_out[0, rows(g)] = result
 
         @pl.when(jnp.logical_and(g == 0, has_left))
         def _():
@@ -247,17 +275,25 @@
     def backward(i, carry):
         g = groups - 1 - i
 
-        @pl.when(has_down)
-        def _():
-            bwd_copy(g).wait_recv()
-
-        coupled = couple(permuted(bwd_in[g], 1, g), 1, rows(g))
-        full_out[0, rows(g)] = solve(fix_b[rows(g)] - coupled, g)
-
-        @pl.when(has_up)
-        def _():
-            bwd_copy(g).start()
-
+        fixed = fix_b[rows(g)]
+        result = jnp.zeros((GROUP, unk), jnp.float32)
+        for h in reversed(range(halves)):
+            j = g * halves + h
+
+            @pl.when(has_down)
+            def _():
+                bwd_copy(j).wait_recv()
+
+            coupled = couple(permuted(bwd_in[j], 1, g), 1, rows(g))
+            solved = solve(fixed - coupled, g, h)
+            bwd_snd[j] = solved[h * BLOCK : (h + 1) * BLOCK]
+
+            @pl.when(has_up)
+            def _():
+                bwd_copy(j).start()
+
+            result = result + solved
+        full_out[0, rows(g)] = result
         return carry
 
     lax.fori_loop(0, groups, backward, 0)
@@ -273,7 +309,7 @@
 
         return carry
 
-    lax.fori_loop(0, groups, drain, 0)
+    lax.fori_loop(0, groups * halves, drain, 0)
 
     @pl.when(has_right)
     def _():
@@ -294,17 +330,26 @@
     wide = -(-unk // 128) * 128
     groups = elems // GROUP
     vmem = pl.BlockSpec(memory_space=pltpu.VMEM)
+    hbm = pl.BlockSpec(memory_space=pltpu.HBM)
+    blocks = elems // BLOCK
+    jacobian = jnp.transpose(flux_jacobian[0], (2, 1, 0))
     f32 = jnp.float32
     dma = pltpu.SemaphoreType.DMA
     return pl.pallas_call(
         functools.partial(sweep_kernel, nf, nc),
         out_shape=(jax.ShapeDtypeStruct(right_side.shape, f32),) * 2,
         in_specs=[
-            vmem, vmem, pl.BlockSpec(memory_space=pl.ANY), vmem, vmem, vmem, vmem,
-            pl.BlockSpec(memory_space=pltpu.SMEM),
+            hbm, hbm, hbm, hbm, hbm, hbm, hbm, hbm,
         ],
         out_specs=(vmem, vmem),
         scratch_shapes=[
+            pltpu.VMEM(right_side.shape, f32),
+            pltpu.VMEM(old_state.shape, f32),
+            pltpu.VMEM(jacobian.shape, f32),
+            pltpu.VMEM(face_lift.shape, f32),
+            pltpu.VMEM(upstream.shape, jnp.int32),
+            pltpu.VMEM(downstream.shape, jnp.int32),
+            pltpu.VMEM(live_counts.shape, jnp.int32),
             pltpu.VMEM((elems, unk, unk), jnp.bfloat16),
             pltpu.VMEM((4, elems, NVAR * wide), f32),
             pltpu.VMEM((4, unk, nb), jnp.bfloat16),
@@ -312,22 +357,24 @@
             pltpu.VMEM((elems + 2 * GROUP, unk), f32),
             pltpu.VMEM((elems, unk), f32),
             pltpu.VMEM((4, GROUP, unk), f32),
-            pltpu.VMEM((groups, GROUP, unk), f32),
-            pltpu.VMEM((groups, GROUP, unk), f32),
+            pltpu.VMEM((blocks, BLOCK, unk), f32),
+            pltpu.VMEM((blocks, BLOCK, unk), f32),
+            pltpu.VMEM((blocks, BLOCK, unk), f32),
+            pltpu.VMEM((blocks, BLOCK, unk), f32),
             pltpu.VMEM((elems, unk), f32),
             pltpu.VMEM((elems, unk), f32),
             pltpu.VMEM((2, elems, 128), f32),
-            dma((groups,)), dma, dma, dma((4,)), dma((4,)),
-            dma((groups,)), dma((groups,)), dma((groups,)), dma((groups,)),
+            dma((7,)), dma((groups,)), dma, dma, dma((4,)), dma((4,)),
+            dma((blocks,)), dma((blocks,)), dma((blocks,)), dma((blocks,)),
         ],
         compiler_params=pltpu.CompilerParams(
-            collective_id=0, has_side_effects=True, vmem_limit_bytes=40 * 1024 * 1024
+            collective_id=0, has_side_effects=True, vmem_limit_bytes=VMEM_BYTES
         ),
         cost_estimate=pl.CostEstimate(
             flops=4 * elems * unk * unk, bytes_accessed=2 * elems * unk * unk, transcendentals=0
         ),
         name="sweep",
-    )(right_side, old_state, block_inverse, flux_jacobian, face_lift, upstream, downstream, live_counts)
+    )(right_side, old_state, block_inverse, jacobian, face_lift, upstream, downstream, live_counts)
 
 
 def solution(mesh):

time: 84.8 us -> 83.7 us (0.987)
  local copies, waits for them, and re-layouts: 6.2 us -> 3.08 us
  Pallas kernels: 77 us -> 79.2 us
    unnamed x13 -> x2, local copies, waits for them, and re-layouts: 6.2 us -> 3.08 us
    pallas_call x1, Pallas kernels: 77 us -> 79.2 us  [per_device(): pl.pallas_call(functools.partial(sweep_kernel, nf, nc), out_shape=(jax.Sh...]
where the time goes in v2:
time: 83.7 us; the launch traced here: 83.6 us
  Pallas kernels  79.2 us (95%)
  local copies, waits for them, and re-layouts  3.08 us (4%)
  between operations  1.29 us (2%)
    pallas_call x1, Pallas kernels, per_device(): pl.pallas_call(functools.partial(sweep_kernel, nf, nc), out_shape=(jax.Sh...  79.2 us
    unnamed x2, local copies, waits for them, and re-layouts  3.08 us

profile of v2, /device:TPU:0, one launch (start us, length us, event | category | flops | bytes accessed | tf_op | source)
XLA Modules:
  0.0 83.6 jit_solution(12199841040039174966)
XLA Ops:
  1.3 79.2 %sweep.1 = (f32[1,64,320]{2,1,0:T(8,128)}, f32[1,64,320]{2,1,0:T(8,128)}) custom-call(f32[1,64,320]{2,1,0:T(8,128)} %rhs_hbm.1, f32[1,64,320]{2,1,0:T(8,128)} %old_hbm.1, bf16[1,64,320,320]{3,2,1,0:T(8,128)(2,1)} %ainv.1, f32[25,4,64]{2,1,0:T(4,128)} %bitcast.3, f32[4,64,64]{2,1,0:T(8,128)} %lift_hbm.1, s32[1,64]{1,0:T(1,128)} %up_hbm.1, s32[1,64]{1,0:T(1,128)} %down_hbm.1, ...), custom_call_target="tpu_custom_call" | custom-call | flops 26214400 | bytes 13107200 | tf_op jit(solution)/shard_map/sweep/pallas_call | solution.py:338
  80.5 1.5 %copy.13 = f32[1,64,320]{2,1,0:T(8,128)} copy(f32[1,64,320]{2,1,0:T(8,128)} %get-tuple-element.4) | data formatting | bytes 163840
  82.0 1.5 %copy.14 = f32[1,64,320]{2,1,0:T(8,128)} copy(f32[1,64,320]{2,1,0:T(8,128)} %get-tuple-element.5) | data formatting | bytes 163840

commit v3 on v2

--- a/solution.py
+++ b/solution.py
@@ -168,7 +168,7 @@
             total = term if total is None else total + term
         return total
 
-    def solve(resid, g, h):
+    def solve(resid, g, h, beside):
         flat = resid.astype(jnp.bfloat16)
         out = jnp.zeros((GROUP, unk), jnp.float32)
         for k in range(h * BLOCK, (h + 1) * BLOCK):
@@ -176,7 +176,9 @@
                 flat, a_vm[g * GROUP + k], CONTRACT_LAST, preferred_element_type=jnp.float32
             )
             out = jnp.where(row == k, product, out)
-        return jnp.where(row + g * GROUP < count, out, 0.0)
+            if k == h * BLOCK:
+                other = beside()
+        return jnp.where(row + g * GROUP < count, out, 0.0), other
 
     @pl.when(has_left)
     def _():
@@ -220,21 +222,30 @@
     lax.fori_loop(0, groups, arrange, 0)
     fix_f[...] = fix_f[...] - couple(oldp[pl.ds(0, elems)], 1, whole)
 
-    def forward(g, carry):
+    def forward_coupling(j, g):
+        return couple(permuted(fwd_in[j], 0, g), 0, rows(g))
+
+    def backward_coupling(j, g):
+        return couple(permuted(bwd_in[j], 1, g), 1, rows(g))
+
+    def forward(g, coupled):
         a_copy(g).wait()
-
         fixed = fix_f[rows(g)]
         coupling = jnp.zeros((GROUP, unk), jnp.float32)
         result = jnp.zeros((GROUP, unk), jnp.float32)
         for h in range(halves):
             j = g * halves + h
-
-            @pl.when(has_up)
+            last = h == halves - 1
+            g_next = jnp.minimum(g + 1, groups - 1) if last else g
+            j_next = g_next * halves if last else j + 1
+
+            @pl.when(jnp.logical_and(has_up, g < groups - 1) if last else has_up)
             def _():
-                fwd_copy(j).wait_recv()
-
-            coupled = couple(permuted(fwd_in[j], 0, g), 0, rows(g))
-            solved = solve(fixed - coupled, g, h)
+                fwd_copy(j_next).wait_recv()
+
+            solved, coupled_next = solve(
+                fixed - coupled, g, h, functools.partial(forward_coupling, j_next, g_next)
+            )
             fwd_snd[j] = solved[h * BLOCK : (h + 1) * BLOCK]
 
             @pl.when(has_down)
@@ -243,6 +254,7 @@
 
             coupling = jnp.where(row // BLOCK == h, coupled, coupling)
             result = result + solved
+            coupled = coupled_next
         fix_b[rows(g)] = rhs[0, rows(g)] - coupling
         halfp[padded_rows(g)] = result
         half_out[0, rows(g)] = result
@@ -251,41 +263,59 @@
         def _():
             halo_copy(halfp, 1, 3, left_dev).start()
 
-        return carry
-
-    lax.fori_loop(0, groups, forward, 0)
+        return coupled
+
+    @pl.when(has_up)
+    def _():
+        fwd_copy(0).wait_recv()
+
+    lax.fori_loop(0, groups, forward, forward_coupling(0, 0))
 
     @pl.when(has_right)
     def _():
         halo_copy(halfp, 0, 2, right_dev).start()
         halo_copy(halfp, 1, 3, left_dev).wait_recv()
 
-    @pl.when(has_left)
-    def _():
-        halo_copy(halfp, 0, 2, right_dev).wait_recv()
-
-    halfp[pl.ds(0, GROUP)] = halo[2]
     halfp[pl.ds(elems + GROUP, GROUP)] = halo[3]
-    fix_b[...] = (
-        fix_b[...]
-        - couple(halfp[pl.ds(GROUP - 1, elems)], 2, whole)
-        - couple(halfp[pl.ds(GROUP + 1, elems)], 3, whole)
+    later = pl.ds(GROUP, elems - GROUP)
+    fix_b[later] = (
+        fix_b[later]
+        - couple(halfp[pl.ds(2 * GROUP - 1, elems - GROUP)], 2, later)
+        - couple(halfp[pl.ds(2 * GROUP + 1, elems - GROUP)], 3, later)
     )
 
-    def backward(i, carry):
+    def backward(i, coupled):
         g = groups - 1 - i
+
+        @pl.when(g == 0)
+        def _():
+            @pl.when(has_left)
+            def _():
+                halo_copy(halfp, 0, 2, right_dev).wait_recv()
+
+            halfp[pl.ds(0, GROUP)] = halo[2]
+            first = pl.ds(0, GROUP)
+            fix_b[first] = (
+                fix_b[first]
+                - couple(halfp[pl.ds(GROUP - 1, GROUP)], 2, first)
+                - couple(halfp[pl.ds(GROUP + 1, GROUP)], 3, first)
+            )
 
         fixed = fix_b[rows(g)]
         result = jnp.zeros((GROUP, unk), jnp.float32)
         for h in reversed(range(halves)):
             j = g * halves + h
-
-            @pl.when(has_down)
+            last = h == 0
+            g_next = jnp.maximum(g - 1, 0) if last else g
+            j_next = g_next * halves + (halves - 1 if last else h - 1)
+
+            @pl.when(jnp.logical_and(has_down, g > 0) if last else has_down)
             def _():
-                bwd_copy(j).wait_recv()
-
-            coupled = couple(permuted(bwd_in[j], 1, g), 1, rows(g))
-            solved = solve(fixed - coupled, g, h)
+                bwd_copy(j_next).wait_recv()
+
+            solved, coupled_next = solve(
+                fixed - coupled, g, h, functools.partial(backward_coupling, j_next, g_next)
+            )
             bwd_snd[j] = solved[h * BLOCK : (h + 1) * BLOCK]
 
             @pl.when(has_up)
@@ -293,10 +323,15 @@
                 bwd_copy(j).start()
 
             result = result + solved
+            coupled = coupled_next
         full_out[0, rows(g)] = result
-        return carry
-
-    lax.fori_loop(0, groups, backward, 0)
+        return coupled
+
+    @pl.when(has_down)
+    def _():
+        bwd_copy(groups * halves - 1).wait_recv()
+
+    lax.fori_loop(0, groups, backward, backward_coupling(groups * halves - 1, groups - 1))
 
     def drain(g, carry):
         @pl.when(has_down)

time: 83.7 us -> 87.6 us (1.047)
  Pallas kernels: 79.2 us -> 83.1 us
    pallas_call x1, Pallas kernels: 79.2 us -> 83.1 us  [per_device(): pl.pallas_call(functools.partial(sweep_kernel, nf, nc), out_shape=(jax.Sh...]
where the time goes in v3:
time: 87.6 us; the launch traced here: 87.4 us
  Pallas kernels  83.1 us (95%)
  local copies, waits for them, and re-layouts  3.08 us (4%)
  between operations  1.29 us (1%)
    pallas_call x1, Pallas kernels, per_device(): pl.pallas_call(functools.partial(sweep_kernel, nf, nc), out_shape=(jax.Sh...  83.1 us
    unnamed x2, local copies, waits for them, and re-layouts  3.08 us

profile of v3, /device:TPU:0, one launch (start us, length us, event | category | flops | bytes accessed | tf_op | source)
XLA Modules:
  0.0 87.4 jit_solution(8434430338500150750)
XLA Ops:
  1.3 83.1 %sweep.1 = (f32[1,64,320]{2,1,0:T(8,128)}, f32[1,64,320]{2,1,0:T(8,128)}) custom-call(f32[1,64,320]{2,1,0:T(8,128)} %rhs_hbm.1, f32[1,64,320]{2,1,0:T(8,128)} %old_hbm.1, bf16[1,64,320,320]{3,2,1,0:T(8,128)(2,1)} %ainv.1, f32[25,4,64]{2,1,0:T(4,128)} %bitcast.3, f32[4,64,64]{2,1,0:T(8,128)} %lift_hbm.1, s32[1,64]{1,0:T(1,128)} %up_hbm.1, s32[1,64]{1,0:T(1,128)} %down_hbm.1, ...), custom_call_target="tpu_custom_call" | custom-call | flops 26214400 | bytes 13107200 | tf_op jit(solution)/shard_map/sweep/pallas_call | solution.py:373
  84.3 1.5 %copy.13 = f32[1,64,320]{2,1,0:T(8,128)} copy(f32[1,64,320]{2,1,0:T(8,128)} %get-tuple-element.4) | data formatting | bytes 163840
  85.9 1.5 %copy.14 = f32[1,64,320]{2,1,0:T(8,128)} copy(f32[1,64,320]{2,1,0:T(8,128)} %get-tuple-element.5) | data formatting | bytes 163840

commit v4 on v2

--- a/solution.py
+++ b/solution.py
@@ -21,14 +21,16 @@
     rhs_hbm, old_hbm, ainv, jac_hbm, lift_hbm, up_hbm, down_hbm, cnt_hbm,
     half_out, full_out,
     rhs, old, jac, lift, up, down, cnt,
-    a_vm, jx, lt, oldp, halfp, down_in, halo, fwd_in, bwd_in, fwd_snd, bwd_snd, fix_f, fix_b, rel,
-    in_sem, a_sem, old_send, old_recv, halo_send, halo_recv, fwd_send, fwd_recv, bwd_send, bwd_recv,
+    a_vm, jx, lt, oldp, result, down_in, halo, inbox, outbox, fix, rel,
+    in_sem, a_sem, old_send, old_recv, halo_send, halo_recv, box_send, box_recv,
 ):
     elems, unk = rhs.shape[1], rhs.shape[2]
     halves = GROUP // BLOCK
     nb = unk // NVAR
     wide = -(-unk // 128) * 128
     groups = elems // GROUP
+    blocks = elems // BLOCK
+    halfp = result.at[0]
     f = lax.axis_index("flow")
     c = lax.axis_index("cross")
     has_up, has_down = f > 0, f < nf - 1
@@ -59,11 +61,8 @@
         start = elems if which == 0 else GROUP
         return remote(buf.at[pl.ds(start, GROUP)], halo.at[slot], halo_send.at[slot], halo_recv.at[slot], dev)
 
-    def fwd_copy(g):
-        return remote(fwd_snd.at[g], fwd_in.at[g], fwd_send.at[g], fwd_recv.at[g], down_dev)
-
-    def bwd_copy(g):
-        return remote(bwd_snd.at[g], bwd_in.at[g], bwd_send.at[g], bwd_recv.at[g], up_dev)
+    def box_copy(slot, dev):
+        return remote(outbox.at[slot], inbox.at[slot], box_send.at[slot], box_recv.at[slot], dev)
 
     sources = (old_hbm, cnt_hbm, jac_hbm, lift_hbm, up_hbm, down_hbm, rhs_hbm)
     fetches = [
@@ -105,12 +104,12 @@
 
     @pl.when(jnp.logical_not(has_up))
     def _():
-        fwd_in[...] = jnp.zeros_like(fwd_in)
+        inbox[pl.ds(0, blocks)] = jnp.zeros((blocks, BLOCK, unk), jnp.float32)
 
     @pl.when(jnp.logical_not(has_down))
     def _():
         down_in[...] = jnp.zeros_like(down_in)
-        bwd_in[...] = jnp.zeros_like(bwd_in)
+        inbox[pl.ds(blocks, blocks)] = jnp.zeros((blocks, BLOCK, unk), jnp.float32)
 
     @pl.when(jnp.logical_not(has_left))
     def _():
@@ -168,148 +167,157 @@
             total = term if total is None else total + term
         return total
 
-    def solve(resid, g, h):
+    def solve(resid, j):
         flat = resid.astype(jnp.bfloat16)
+        first = (j % halves) * BLOCK
         out = jnp.zeros((GROUP, unk), jnp.float32)
-        for k in range(h * BLOCK, (h + 1) * BLOCK):
+        for k in range(BLOCK):
             product = lax.dot_general(
-                flat, a_vm[g * GROUP + k], CONTRACT_LAST, preferred_element_type=jnp.float32
+                flat, a_vm[j * BLOCK + k], CONTRACT_LAST, preferred_element_type=jnp.float32
             )
-            out = jnp.where(row == k, product, out)
-        return jnp.where(row + g * GROUP < count, out, 0.0)
-
-    @pl.when(has_left)
-    def _():
-        halo_copy(oldp, 0, 0, right_dev).wait_recv()
-
-    @pl.when(has_right)
-    def _():
-        halo_copy(oldp, 1, 1, left_dev).wait_recv()
-
-    oldp[pl.ds(0, GROUP)] = halo[0]
-    oldp[pl.ds(elems + GROUP, GROUP)] = halo[1]
-
-    whole = pl.ds(0, elems)
-    fix_f[...] = (
-        rhs[0]
-        - couple(oldp[pl.ds(GROUP - 1, elems)], 2, whole)
-        - couple(oldp[pl.ds(GROUP + 1, elems)], 3, whole)
-    )
-
-    @pl.when(has_down)
-    def _():
-        old_copy().wait_recv()
-
-    def arrange(g, carry):
-        x = down_in[rows(g)]
-        oldp[rows(g)] = jnp.where(row < BLOCK, permuted(x[:BLOCK], 1, g), permuted(x[BLOCK:], 1, g))
+            out = jnp.where(row == first + k, product, out)
+        return jnp.where(row + (j // halves) * GROUP < count, out, 0.0)
+
+    def prepare_forward():
+        @pl.when(has_left)
+        def _():
+            halo_copy(oldp, 0, 0, right_dev).wait_recv()
+
+        @pl.when(has_right)
+        def _():
+            halo_copy(oldp, 1, 1, left_dev).wait_recv()
+
+        oldp[pl.ds(0, GROUP)] = halo[0]
+        oldp[pl.ds(elems + GROUP, GROUP)] = halo[1]
+
+        whole = pl.ds(0, elems)
+        sides = couple(oldp[pl.ds(GROUP - 1, elems)], 2, whole) + couple(
+            oldp[pl.ds(GROUP + 1, elems)], 3, whole
+        )
+
+        @pl.when(has_down)
+        def _():
+            old_copy().wait_recv()
+
+        @pl.when(has_up)
+        def _():
+            old_copy().wait_send()
+
+        @pl.when(has_right)
+        def _():
+            halo_copy(oldp, 0, 0, right_dev).wait_send()
+
+        @pl.when(has_left)
+        def _():
+            halo_copy(oldp, 1, 1, left_dev).wait_send()
+
+        for g in range(groups):
+            x = down_in[pl.ds(g * GROUP, GROUP)]
+            oldp[pl.ds(g * GROUP, GROUP)] = jnp.where(
+                row < BLOCK, permuted(x[:BLOCK], 1, g), permuted(x[BLOCK:], 1, g)
+            )
+        fix[0] = rhs[0] - sides - couple(oldp[pl.ds(0, elems)], 1, whole)
+
+    def prepare_backward():
+        @pl.when(has_right)
+        def _():
+            halo_copy(halfp, 0, 2, right_dev).start()
+            halo_copy(halfp, 1, 3, left_dev).wait_recv()
+
+        halfp[pl.ds(elems + GROUP, GROUP)] = halo[3]
+        later = pl.ds(GROUP, elems - GROUP)
+        fix[1, later] = (
+            fix[1, later]
+            - couple(halfp[pl.ds(2 * GROUP - 1, elems - GROUP)], 2, later)
+            - couple(halfp[pl.ds(2 * GROUP + 1, elems - GROUP)], 3, later)
+        )
+
+    def prepare_first_group():
+        @pl.when(has_left)
+        def _():
+            halo_copy(halfp, 0, 2, right_dev).wait_recv()
+
+        halfp[pl.ds(0, GROUP)] = halo[2]
+        first = pl.ds(0, GROUP)
+        fix[1, first] = (
+            fix[1, first]
+            - couple(halfp[pl.ds(GROUP - 1, GROUP)], 2, first)
+            - couple(halfp[pl.ds(GROUP + 1, GROUP)], 3, first)
+        )
+
+    def step(t, carry):
+        done = jnp.maximum(t - 1, 0)
+        phase = done // blocks
+        u = done % blocks
+        j = phase * (blocks - 1) + (1 - 2 * phase) * u
+        g = j // halves
+        slot = phase * blocks + j + (1 - jnp.minimum(t, 1)) * (2 * blocks)
+        forward = jnp.logical_and(t > 0, phase == 0)
+        backward = phase == 1
+
+        @pl.when(t == 1)
+        def _():
+            prepare_forward()
+
+        @pl.when(t == blocks + 1)
+        def _():
+            prepare_backward()
+
+        @pl.when(t == 2 * blocks + 1 - halves)
+        def _():
+            prepare_first_group()
+
+        @pl.when(jnp.logical_or(t == 0, jnp.logical_and(jnp.logical_and(forward, t > 1), u % halves == 0)))
+        def _():
+            a_copy(g).wait()
+
+        @pl.when(jnp.logical_or(jnp.logical_and(forward, has_up), jnp.logical_and(backward, has_down)))
+        def _():
+            box_copy(slot, up_dev).wait_recv()
+
+        coupled = couple(permuted(inbox[slot], phase, g), phase, rows(g))
+        solved = solve(fix[phase, rows(g)] - coupled, j)
+        half = j % halves
+        outbox[slot] = jnp.where(half == 0, solved[:BLOCK], solved[BLOCK:])
+
+        @pl.when(jnp.logical_and(forward, has_down))
+        def _():
+            box_copy(slot, down_dev).start()
+
+        @pl.when(jnp.logical_and(backward, has_up))
+        def _():
+            box_copy(slot, up_dev).start()
+
+        fresh = u % halves == 0
+        result[phase, padded_rows(g)] = jnp.where(fresh, 0.0, result[phase, padded_rows(g)]) + solved
+
+        @pl.when(phase == 0)
+        def _():
+            base = jnp.where(fresh, rhs[0, rows(g)], fix[1, rows(g)])
+            fix[1, rows(g)] = base - jnp.where(row // BLOCK == half, coupled, 0.0)
+
+        @pl.when(jnp.logical_and(t == halves, has_left))
+        def _():
+            halo_copy(halfp, 1, 3, left_dev).start()
+
         return carry
 
-    @pl.when(has_up)
-    def _():
-        old_copy().wait_send()
-
-    @pl.when(has_right)
-    def _():
-        halo_copy(oldp, 0, 0, right_dev).wait_send()
-
-    @pl.when(has_left)
-    def _():
-        halo_copy(oldp, 1, 1, left_dev).wait_send()
-
-    lax.fori_loop(0, groups, arrange, 0)
-    fix_f[...] = fix_f[...] - couple(oldp[pl.ds(0, elems)], 1, whole)
-
-    def forward(g, carry):
-        a_copy(g).wait()
-
-        fixed = fix_f[rows(g)]
-        coupling = jnp.zeros((GROUP, unk), jnp.float32)
-        result = jnp.zeros((GROUP, unk), jnp.float32)
-        for h in range(halves):
-            j = g * halves + h
-
-            @pl.when(has_up)
-            def _():
-                fwd_copy(j).wait_recv()
-
-            coupled = couple(permuted(fwd_in[j], 0, g), 0, rows(g))
-            solved = solve(fixed - coupled, g, h)
-            fwd_snd[j] = solved[h * BLOCK : (h + 1) * BLOCK]
-
-            @pl.when(has_down)
-            def _():
-                fwd_copy(j).start()
-
-            coupling = jnp.where(row // BLOCK == h, coupled, coupling)
-            result = result + solved
-        fix_b[rows(g)] = rhs[0, rows(g)] - coupling
-        halfp[padded_rows(g)] = result
-        half_out[0, rows(g)] = result
-
-        @pl.when(jnp.logical_and(g == 0, has_left))
-        def _():
-            halo_copy(halfp, 1, 3, left_dev).start()
+    lax.fori_loop(0, 2 * blocks + 1, step, 0)
+    half_out[0] = result[0, pl.ds(GROUP, elems)]
+    full_out[0] = result[1, pl.ds(GROUP, elems)]
+
+    def drain(j, carry):
+        @pl.when(has_down)
+        def _():
+            box_copy(j, down_dev).wait_send()
+
+        @pl.when(has_up)
+        def _():
+            box_copy(blocks + j, up_dev).wait_send()
 
         return carry
 
-    lax.fori_loop(0, groups, forward, 0)
-
-    @pl.when(has_right)
-    def _():
-        halo_copy(halfp, 0, 2, right_dev).start()
-        halo_copy(halfp, 1, 3, left_dev).wait_recv()
-
-    @pl.when(has_left)
-    def _():
-        halo_copy(halfp, 0, 2, right_dev).wait_recv()
-
-    halfp[pl.ds(0, GROUP)] = halo[2]
-    halfp[pl.ds(elems + GROUP, GROUP)] = halo[3]
-    fix_b[...] = (
-        fix_b[...]
-        - couple(halfp[pl.ds(GROUP - 1, elems)], 2, whole)
-        - couple(halfp[pl.ds(GROUP + 1, elems)], 3, whole)
-    )
-
-    def backward(i, carry):
-        g = groups - 1 - i
-
-        fixed = fix_b[rows(g)]
-        result = jnp.zeros((GROUP, unk), jnp.float32)
-        for h in reversed(range(halves)):
-            j = g * halves + h
-
-            @pl.when(has_down)
-            def _():
-                bwd_copy(j).wait_recv()
-
-            coupled = couple(permuted(bwd_in[j], 1, g), 1, rows(g))
-            solved = solve(fixed - coupled, g, h)
-            bwd_snd[j] = solved[h * BLOCK : (h + 1) * BLOCK]
-
-            @pl.when(has_up)
-            def _():
-                bwd_copy(j).start()
-
-            result = result + solved
-        full_out[0, rows(g)] = result
-        return carry
-
-    lax.fori_loop(0, groups, backward, 0)
-
-    def drain(g, carry):
-        @pl.when(has_down)
-        def _():
-            fwd_copy(g).wait_send()
-
-        @pl.when(has_up)
-        def _():
-            bwd_copy(g).wait_send()
-
-        return carry
-
-    lax.fori_loop(0, groups * halves, drain, 0)
+    lax.fori_loop(0, blocks, drain, 0)
 
     @pl.when(has_right)
     def _():
@@ -354,18 +362,15 @@
             pltpu.VMEM((4, elems, NVAR * wide), f32),
             pltpu.VMEM((4, unk, nb), jnp.bfloat16),
             pltpu.VMEM((elems + 2 * GROUP, unk), f32),
-            pltpu.VMEM((elems + 2 * GROUP, unk), f32),
+            pltpu.VMEM((2, elems + 2 * GROUP, unk), f32),
             pltpu.VMEM((elems, unk), f32),
             pltpu.VMEM((4, GROUP, unk), f32),
-            pltpu.VMEM((blocks, BLOCK, unk), f32),
-            pltpu.VMEM((blocks, BLOCK, unk), f32),
-            pltpu.VMEM((blocks, BLOCK, unk), f32),
-            pltpu.VMEM((blocks, BLOCK, unk), f32),
-            pltpu.VMEM((elems, unk), f32),
-            pltpu.VMEM((elems, unk), f32),
+            pltpu.VMEM((2 * blocks + 1, BLOCK, unk), f32),
+            pltpu.VMEM((2 * blocks + 1, BLOCK, unk), f32),
+            pltpu.VMEM((2, elems, unk), f32),
             pltpu.VMEM((2, elems, 128), f32),
             dma((7,)), dma((groups,)), dma, dma, dma((4,)), dma((4,)),
-            dma((blocks,)), dma((blocks,)), dma((blocks,)), dma((blocks,)),
+            dma((2 * blocks,)), dma((2 * blocks,)),
         ],
         compiler_params=pltpu.CompilerParams(
             collective_id=0, has_side_effects=True, vmem_limit_bytes=VMEM_BYTES

time: 83.7 us -> 84.4 us (level)
  no operation moved by 1% of the time
where the time goes in v4:
time: 84.4 us; the launch traced here: 84.2 us
  Pallas kernels  79.9 us (95%)
  local copies, waits for them, and re-layouts  3.08 us (4%)
  between operations  1.29 us (2%)
    pallas_call x1, Pallas kernels, per_device(): pl.pallas_call(functools.partial(sweep_kernel, nf, nc), out_shape=(jax.Sh...  79.9 us
    unnamed x2, local copies, waits for them, and re-layouts  3.08 us

profile of v4, /device:TPU:0, one launch (start us, length us, event | category | flops | bytes accessed | tf_op | source)
XLA Modules:
  0.0 84.2 jit_solution(4537870998598329748)
XLA Ops:
  1.3 79.9 %sweep.1 = (f32[1,64,320]{2,1,0:T(8,128)}, f32[1,64,320]{2,1,0:T(8,128)}) custom-call(f32[1,64,320]{2,1,0:T(8,128)} %rhs_hbm.1, f32[1,64,320]{2,1,0:T(8,128)} %old_hbm.1, bf16[1,64,320,320]{3,2,1,0:T(8,128)(2,1)} %ainv.1, f32[25,4,64]{2,1,0:T(4,128)} %bitcast.3, f32[4,64,64]{2,1,0:T(8,128)} %lift_hbm.1, s32[1,64]{1,0:T(1,128)} %up_hbm.1, s32[1,64]{1,0:T(1,128)} %down_hbm.1, ...), custom_call_target="tpu_custom_call" | custom-call | flops 26214400 | bytes 13107200 | tf_op jit(solution)/shard_map/sweep/pallas_call | solution.py:346
  81.2 1.5 %copy.13 = f32[1,64,320]{2,1,0:T(8,128)} copy(f32[1,64,320]{2,1,0:T(8,128)} %get-tuple-element.4) | data formatting | bytes 163840
  82.7 1.5 %copy.14 = f32[1,64,320]{2,1,0:T(8,128)} copy(f32[1,64,320]{2,1,0:T(8,128)} %get-tuple-element.5) | data formatting | bytes 163840

commit v5 on v4

--- a/solution.py
+++ b/solution.py
@@ -21,7 +21,7 @@
     rhs_hbm, old_hbm, ainv, jac_hbm, lift_hbm, up_hbm, down_hbm, cnt_hbm,
     half_out, full_out,
     rhs, old, jac, lift, up, down, cnt,
-    a_vm, jx, lt, oldp, result, down_in, halo, inbox, outbox, fix, rel,
+    a_vm, jx, lt, oldp, result, down_in, halo, inbox, outbox, fix, rel, packed, ahead,
     in_sem, a_sem, old_send, old_recv, halo_send, halo_recv, box_send, box_recv,
 ):
     elems, unk = rhs.shape[1], rhs.shape[2]
@@ -31,6 +31,8 @@
     groups = elems // GROUP
     blocks = elems // BLOCK
     halfp = result.at[0]
+    main = unk - unk // NVAR
+    rest = unk - main
     f = lax.axis_index("flow")
     c = lax.axis_index("cross")
     has_up, has_down = f > 0, f < nf - 1
@@ -167,16 +169,35 @@
             total = term if total is None else total + term
         return total
 
-    def solve(resid, j):
-        flat = resid.astype(jnp.bfloat16)
+    def solve(resid, j, beside):
         first = (j % halves) * BLOCK
+        tail = jnp.concatenate([resid[:, main:]] * BLOCK, axis=1)
+        lane = lax.broadcasted_iota(jnp.int32, (GROUP, BLOCK * rest), 1)
+        line = lax.broadcasted_iota(jnp.int32, (GROUP, BLOCK * rest), 0)
+        tail = jnp.where(lane // rest == line % BLOCK, tail, 0.0).astype(jnp.bfloat16)
+        head = resid[:, :main].astype(jnp.bfloat16)
         out = jnp.zeros((GROUP, unk), jnp.float32)
         for k in range(BLOCK):
             product = lax.dot_general(
-                flat, a_vm[j * BLOCK + k], CONTRACT_LAST, preferred_element_type=jnp.float32
+                head, a_vm[j * BLOCK + k, :, 0:main], CONTRACT_LAST, preferred_element_type=jnp.float32
             )
             out = jnp.where(row == first + k, product, out)
-        return jnp.where(row + (j // halves) * GROUP < count, out, 0.0)
+            if k == 0:
+                other = beside()
+        out = out + lax.dot_general(tail, packed[j], CONTRACT_LAST, preferred_element_type=jnp.float32)
+        mine = jnp.logical_and(row // BLOCK == j % halves, row + (j // halves) * GROUP < count)
+        return jnp.where(mine, out, 0.0), other
+
+    def pack(j, carry):
+        packed[j] = jnp.concatenate([a_vm[j * BLOCK + k, :, main:] for k in range(BLOCK)], axis=1)
+        return carry
+
+    def wait_a(g, carry):
+        a_copy(g).wait()
+        return carry
+
+    lax.fori_loop(0, groups, wait_a, 0)
+    lax.fori_loop(0, blocks, pack, 0)
 
     def prepare_forward():
         @pl.when(has_left)
@@ -244,6 +265,9 @@
             - couple(halfp[pl.ds(GROUP - 1, GROUP)], 2, first)
             - couple(halfp[pl.ds(GROUP + 1, GROUP)], 3, first)
         )
+
+    def coupling(slot, phase, g):
+        return couple(permuted(inbox[slot], phase, g), phase, rows(g))
 
     def step(t, carry):
         done = jnp.maximum(t - 1, 0)
@@ -267,16 +291,30 @@
         def _():
             prepare_first_group()
 
-        @pl.when(jnp.logical_or(t == 0, jnp.logical_and(jnp.logical_and(forward, t > 1), u % halves == 0)))
-        def _():
-            a_copy(g).wait()
-
-        @pl.when(jnp.logical_or(jnp.logical_and(forward, has_up), jnp.logical_and(backward, has_down)))
-        def _():
-            box_copy(slot, up_dev).wait_recv()
-
-        coupled = couple(permuted(inbox[slot], phase, g), phase, rows(g))
-        solved = solve(fix[phase, rows(g)] - coupled, j)
+        inbound = jnp.logical_or(jnp.logical_and(forward, has_up), jnp.logical_and(backward, has_down))
+        opening = jnp.logical_and(t > 0, u == 0)
+        following = jnp.logical_and(u > 0, u < blocks - 1)
+        direction = 1 - 2 * phase
+        g_next = jnp.clip(j + direction, 0, blocks - 1) // halves
+
+        @pl.when(opening)
+        def _():
+            @pl.when(inbound)
+            def _():
+                box_copy(slot, up_dev).wait_recv()
+
+            ahead[...] = coupling(slot, phase, g)
+
+        @pl.when(jnp.logical_and(following, inbound))
+        def _():
+            box_copy(slot + direction, up_dev).wait_recv()
+
+        ok = following.astype(jnp.int32)
+        slot_next = ok * (slot + direction) + (1 - ok) * (2 * blocks)
+        coupled = ahead[...]
+        solved, coupled_next = solve(
+            fix[phase, rows(g)] - coupled, j, lambda: coupling(slot_next, phase, g_next)
+        )
         half = j % halves
         outbox[slot] = jnp.where(half == 0, solved[:BLOCK], solved[BLOCK:])
 
@@ -287,6 +325,16 @@
         @pl.when(jnp.logical_and(backward, has_up))
         def _():
             box_copy(slot, up_dev).start()
+
+        ahead[...] = coupled_next
+
+        @pl.when(opening)
+        def _():
+            @pl.when(inbound)
+            def _():
+                box_copy(slot + direction, up_dev).wait_recv()
+
+            ahead[...] = coupling(slot + direction, phase, g_next)
 
         fresh = u % halves == 0
         result[phase, padded_rows(g)] = jnp.where(fresh, 0.0, result[phase, padded_rows(g)]) + solved
@@ -369,6 +417,8 @@
             pltpu.VMEM((2 * blocks + 1, BLOCK, unk), f32),
             pltpu.VMEM((2, elems, unk), f32),
             pltpu.VMEM((2, elems, 128), f32),
+            pltpu.VMEM((blocks, unk, BLOCK * (unk // NVAR)), jnp.bfloat16),
+            pltpu.VMEM((GROUP, unk), f32),
             dma((7,)), dma((groups,)), dma, dma, dma((4,)), dma((4,)),
             dma((2 * blocks,)), dma((2 * blocks,)),
         ],

time: 84.4 us -> 87.6 us (1.038)
  Pallas kernels: 79.9 us -> 83 us
    pallas_call x1, Pallas kernels: 79.9 us -> 83 us  [per_device(): pl.pallas_call(functools.partial(sweep_kernel, nf, nc), out_shape=(jax.Sh...]
where the time goes in v5:
time: 87.6 us; the launch traced here: 87.4 us
  Pallas kernels  83 us (95%)
  local copies, waits for them, and re-layouts  3.08 us (4%)
  between operations  1.29 us (1%)
    pallas_call x1, Pallas kernels, per_device(): pl.pallas_call(functools.partial(sweep_kernel, nf, nc), out_shape=(jax.Sh...  83 us
    unnamed x2, local copies, waits for them, and re-layouts  3.08 us

profile of v5, /device:TPU:0, one launch (start us, length us, event | category | flops | bytes accessed | tf_op | source)
XLA Modules:
  0.0 87.4 jit_solution(10647300101401904154)
XLA Ops:
  1.3 83.0 %sweep.1 = (f32[1,64,320]{2,1,0:T(8,128)}, f32[1,64,320]{2,1,0:T(8,128)}) custom-call(f32[1,64,320]{2,1,0:T(8,128)} %rhs_hbm.1, f32[1,64,320]{2,1,0:T(8,128)} %old_hbm.1, bf16[1,64,320,320]{3,2,1,0:T(8,128)(2,1)} %ainv.1, f32[25,4,64]{2,1,0:T(4,128)} %bitcast.3, f32[4,64,64]{2,1,0:T(8,128)} %lift_hbm.1, s32[1,64]{1,0:T(1,128)} %up_hbm.1, s32[1,64]{1,0:T(1,128)} %down_hbm.1, ...), custom_call_target="tpu_custom_call" | custom-call | flops 26214400 | bytes 13107200 | tf_op jit(solution)/shard_map/sweep/pallas_call | solution.py:394
  84.3 1.5 %copy.13 = f32[1,64,320]{2,1,0:T(8,128)} copy(f32[1,64,320]{2,1,0:T(8,128)} %get-tuple-element.4) | data formatting | bytes 163840
  85.9 1.5 %copy.14 = f32[1,64,320]{2,1,0:T(8,128)} copy(f32[1,64,320]{2,1,0:T(8,128)} %get-tuple-element.5) | data formatting | bytes 163840

commit v6 on v4

--- a/solution.py
+++ b/solution.py
@@ -9,7 +9,6 @@
 
 NVAR = 5
 GROUP = 8
-BLOCK = 4
 VMEM_BYTES = 64 * 1024 * 1024
 MESH = pl.DeviceIdType.MESH
 CONTRACT_LAST = (((1,), (1,)), ((), ()))
@@ -19,17 +18,16 @@
 def sweep_kernel(
     nf, nc,
     rhs_hbm, old_hbm, ainv, jac_hbm, lift_hbm, up_hbm, down_hbm, cnt_hbm,
-    half_out, full_out,
+    half_hbm, full_hbm,
     rhs, old, jac, lift, up, down, cnt,
-    a_vm, jx, lt, oldp, result, down_in, halo, inbox, outbox, fix, rel,
-    in_sem, a_sem, old_send, old_recv, halo_send, halo_recv, box_send, box_recv,
+    a_vm, jx, lt, oldp, result, down_in, halo, inbox, outbox, fix, rel, coupled_ref,
+    in_sem, out_sem, a_sem, old_send, old_recv, halo_send, halo_recv, box_send, box_recv,
 ):
     elems, unk = rhs.shape[1], rhs.shape[2]
-    halves = GROUP // BLOCK
     nb = unk // NVAR
     wide = -(-unk // 128) * 128
     groups = elems // GROUP
-    blocks = elems // BLOCK
+    blocks = elems // GROUP
     halfp = result.at[0]
     f = lax.axis_index("flow")
     c = lax.axis_index("cross")
@@ -104,12 +102,11 @@
 
     @pl.when(jnp.logical_not(has_up))
     def _():
-        inbox[pl.ds(0, blocks)] = jnp.zeros((blocks, BLOCK, unk), jnp.float32)
+        coupled_ref[...] = edge
 
     @pl.when(jnp.logical_not(has_down))
     def _():
         down_in[...] = jnp.zeros_like(down_in)
-        inbox[pl.ds(blocks, blocks)] = jnp.zeros((blocks, BLOCK, unk), jnp.float32)
 
     @pl.when(jnp.logical_not(has_left))
     def _():
@@ -127,7 +124,7 @@
     square = (elems, elems)
     diagonal = lax.broadcasted_iota(jnp.int32, square, 0) == lax.broadcasted_iota(jnp.int32, square, 1)
     for i, index in enumerate((up, down)):
-        local = (index[...] % BLOCK).astype(jnp.float32)
+        local = (index[...] % GROUP).astype(jnp.float32)
         column = jnp.sum(jnp.where(diagonal, jnp.broadcast_to(local, square), 0.0), axis=1, keepdims=True)
         rel[i] = jnp.broadcast_to(column, (elems, 128))
 
@@ -151,7 +148,7 @@
     def permuted(x, which, g):
         column = rel[which, rows(g)][:, 0:1]
         out = jnp.broadcast_to(x[0:1], (GROUP, unk))
-        for k in range(1, BLOCK):
+        for k in range(1, GROUP):
             out = jnp.where(column == float(k), x[k : k + 1], out)
         return out
 
@@ -169,14 +166,13 @@
 
     def solve(resid, j):
         flat = resid.astype(jnp.bfloat16)
-        first = (j % halves) * BLOCK
         out = jnp.zeros((GROUP, unk), jnp.float32)
-        for k in range(BLOCK):
+        for k in range(GROUP):
             product = lax.dot_general(
-                flat, a_vm[j * BLOCK + k], CONTRACT_LAST, preferred_element_type=jnp.float32
+                flat, a_vm[j * GROUP + k], CONTRACT_LAST, preferred_element_type=jnp.float32
             )
-            out = jnp.where(row == first + k, product, out)
-        return jnp.where(row + (j // halves) * GROUP < count, out, 0.0)
+            out = jnp.where(row == k, product, out)
+        return jnp.where(row + j * GROUP < count, out, 0.0)
 
     def prepare_forward():
         @pl.when(has_left)
@@ -213,9 +209,7 @@
 
         for g in range(groups):
             x = down_in[pl.ds(g * GROUP, GROUP)]
-            oldp[pl.ds(g * GROUP, GROUP)] = jnp.where(
-                row < BLOCK, permuted(x[:BLOCK], 1, g), permuted(x[BLOCK:], 1, g)
-            )
+            oldp[pl.ds(g * GROUP, GROUP)] = permuted(x, 1, g)
         fix[0] = rhs[0] - sides - couple(oldp[pl.ds(0, elems)], 1, whole)
 
     def prepare_backward():
@@ -245,40 +239,45 @@
             - couple(halfp[pl.ds(GROUP + 1, GROUP)], 3, first)
         )
 
+    def half_copy():
+        return pltpu.make_async_copy(result.at[0, pl.ds(GROUP, elems)], half_hbm.at[0], out_sem.at[blocks])
+
+    def full_copy(j):
+        return pltpu.make_async_copy(result.at[1, padded_rows(j)], full_hbm.at[0, rows(j)], out_sem.at[j])
+
     def step(t, carry):
-        done = jnp.maximum(t - 1, 0)
-        phase = done // blocks
-        u = done % blocks
+        phase = t // blocks
+        u = t % blocks
         j = phase * (blocks - 1) + (1 - 2 * phase) * u
-        g = j // halves
-        slot = phase * blocks + j + (1 - jnp.minimum(t, 1)) * (2 * blocks)
-        forward = jnp.logical_and(t > 0, phase == 0)
+        slot = phase * blocks + j
+        forward = phase == 0
         backward = phase == 1
 
-        @pl.when(t == 1)
-        def _():
-            prepare_forward()
-
-        @pl.when(t == blocks + 1)
+        @pl.when(t == blocks)
         def _():
             prepare_backward()
-
-        @pl.when(t == 2 * blocks + 1 - halves)
+            half_copy().start()
+
+            @pl.when(jnp.logical_not(has_down))
+            def _():
+                coupled_ref[...] = edge
+
+        @pl.when(t == 2 * blocks - 1)
         def _():
             prepare_first_group()
 
-        @pl.when(jnp.logical_or(t == 0, jnp.logical_and(jnp.logical_and(forward, t > 1), u % halves == 0)))
-        def _():
-            a_copy(g).wait()
+        @pl.when(forward)
+        def _():
+            a_copy(j).wait()
 
         @pl.when(jnp.logical_or(jnp.logical_and(forward, has_up), jnp.logical_and(backward, has_down)))
         def _():
             box_copy(slot, up_dev).wait_recv()
-
-        coupled = couple(permuted(inbox[slot], phase, g), phase, rows(g))
-        solved = solve(fix[phase, rows(g)] - coupled, j)
-        half = j % halves
-        outbox[slot] = jnp.where(half == 0, solved[:BLOCK], solved[BLOCK:])
+            coupled_ref[...] = couple(permuted(inbox[slot][:, :unk], phase, j), phase, rows(j))
+
+        coupled = coupled_ref[...]
+        solved = solve(fix[phase, rows(j)] - coupled, j)
+        outbox[slot, :, 0:unk] = solved
 
         @pl.when(jnp.logical_and(forward, has_down))
         def _():
@@ -288,23 +287,25 @@
         def _():
             box_copy(slot, up_dev).start()
 
-        fresh = u % halves == 0
-        result[phase, padded_rows(g)] = jnp.where(fresh, 0.0, result[phase, padded_rows(g)]) + solved
-
-        @pl.when(phase == 0)
-        def _():
-            base = jnp.where(fresh, rhs[0, rows(g)], fix[1, rows(g)])
-            fix[1, rows(g)] = base - jnp.where(row // BLOCK == half, coupled, 0.0)
-
-        @pl.when(jnp.logical_and(t == halves, has_left))
+        result[phase, padded_rows(j)] = solved
+
+        @pl.when(forward)
+        def _():
+            fix[1, rows(j)] = rhs[0, rows(j)] - coupled
+
+        @pl.when(backward)
+        def _():
+            full_copy(j).start()
+
+        @pl.when(jnp.logical_and(t == 0, has_left))
         def _():
             halo_copy(halfp, 1, 3, left_dev).start()
 
         return carry
 
-    lax.fori_loop(0, 2 * blocks + 1, step, 0)
-    half_out[0] = result[0, pl.ds(GROUP, elems)]
-    full_out[0] = result[1, pl.ds(GROUP, elems)]
+    outbox[...] = jnp.zeros_like(outbox)
+    prepare_forward()
+    lax.fori_loop(0, 2 * blocks, step, 0)
 
     def drain(j, carry):
         @pl.when(has_down)
@@ -315,9 +316,11 @@
         def _():
             box_copy(blocks + j, up_dev).wait_send()
 
+        full_copy(j).wait()
         return carry
 
     lax.fori_loop(0, blocks, drain, 0)
+    half_copy().wait()
 
     @pl.when(has_right)
     def _():
@@ -337,9 +340,8 @@
     nb = unk // NVAR
     wide = -(-unk // 128) * 128
     groups = elems // GROUP
-    vmem = pl.BlockSpec(memory_space=pltpu.VMEM)
     hbm = pl.BlockSpec(memory_space=pltpu.HBM)
-    blocks = elems // BLOCK
+    blocks = elems // GROUP
     jacobian = jnp.transpose(flux_jacobian[0], (2, 1, 0))
     f32 = jnp.float32
     dma = pltpu.SemaphoreType.DMA
@@ -349,7 +351,7 @@
         in_specs=[
             hbm, hbm, hbm, hbm, hbm, hbm, hbm, hbm,
         ],
-        out_specs=(vmem, vmem),
+        out_specs=(hbm, hbm),
         scratch_shapes=[
             pltpu.VMEM(right_side.shape, f32),
             pltpu.VMEM(old_state.shape, f32),
@@ -365,11 +367,12 @@
             pltpu.VMEM((2, elems + 2 * GROUP, unk), f32),
             pltpu.VMEM((elems, unk), f32),
             pltpu.VMEM((4, GROUP, unk), f32),
-            pltpu.VMEM((2 * blocks + 1, BLOCK, unk), f32),
-            pltpu.VMEM((2 * blocks + 1, BLOCK, unk), f32),
+            pltpu.VMEM((2 * blocks, GROUP, wide), f32),
+            pltpu.VMEM((2 * blocks, GROUP, wide), f32),
             pltpu.VMEM((2, elems, unk), f32),
             pltpu.VMEM((2, elems, 128), f32),
-            dma((7,)), dma((groups,)), dma, dma, dma((4,)), dma((4,)),
+            pltpu.VMEM((GROUP, unk), f32),
+            dma((7,)), dma((blocks + 1,)), dma((groups,)), dma, dma, dma((4,)), dma((4,)),
             dma((2 * blocks,)), dma((2 * blocks,)),
         ],
         compiler_params=pltpu.CompilerParams(

time: 84.4 us -> 82.3 us (0.975)
  Pallas kernels: 79.9 us -> 77.7 us
    pallas_call x1, Pallas kernels: 79.9 us -> 77.7 us  [per_device(): pl.pallas_call(functools.partial(sweep_kernel, nf, nc), out_shape=(jax.Sh...]
where the time goes in v6:
time: 82.3 us; the launch traced here: 82.1 us
  Pallas kernels  77.7 us (94%)
  local copies, waits for them, and re-layouts  3.08 us (4%)
  between operations  1.29 us (2%)
    pallas_call x1, Pallas kernels, per_device(): pl.pallas_call(functools.partial(sweep_kernel, nf, nc), out_shape=(jax.Sh...  77.7 us
    unnamed x2, local copies, waits for them, and re-layouts  3.08 us

profile of v6, /device:TPU:0, one launch (start us, length us, event | category | flops | bytes accessed | tf_op | source)
XLA Modules:
  0.0 82.1 jit_solution(520287835963997351)
XLA Ops:
  1.3 77.7 %sweep.1 = (f32[1,64,320]{2,1,0:T(8,128)}, f32[1,64,320]{2,1,0:T(8,128)}) custom-call(f32[1,64,320]{2,1,0:T(8,128)} %rhs_hbm.1, f32[1,64,320]{2,1,0:T(8,128)} %old_hbm.1, bf16[1,64,320,320]{3,2,1,0:T(8,128)(2,1)} %ainv.1, f32[25,4,64]{2,1,0:T(4,128)} %bitcast.3, f32[4,64,64]{2,1,0:T(8,128)} %lift_hbm.1, s32[1,64]{1,0:T(1,128)} %up_hbm.1, s32[1,64]{1,0:T(1,128)} %down_hbm.1, ...), custom_call_target="tpu_custom_call" | custom-call | flops 26214400 | bytes 13107200 | tf_op jit(solution)/shard_map/sweep/pallas_call | solution.py:348
  79.0 1.5 %copy.13 = f32[1,64,320]{2,1,0:T(8,128)} copy(f32[1,64,320]{2,1,0:T(8,128)} %get-tuple-element.4) | data formatting | bytes 163840
  80.5 1.5 %copy.14 = f32[1,64,320]{2,1,0:T(8,128)} copy(f32[1,64,320]{2,1,0:T(8,128)} %get-tuple-element.5) | data formatting | bytes 163840

commit v7 on v6

--- a/solution.py
+++ b/solution.py
@@ -20,7 +20,7 @@
     rhs_hbm, old_hbm, ainv, jac_hbm, lift_hbm, up_hbm, down_hbm, cnt_hbm,
     half_hbm, full_hbm,
     rhs, old, jac, lift, up, down, cnt,
-    a_vm, jx, lt, oldp, result, down_in, halo, inbox, outbox, fix, rel, coupled_ref,
+    a_vm, jx, lt, oldp, result, down_in, halo, inbox, outbox, fix, rel, live, coupled_ref,
     in_sem, out_sem, a_sem, old_send, old_recv, halo_send, halo_recv, box_send, box_recv,
 ):
     elems, unk = rhs.shape[1], rhs.shape[2]
@@ -82,7 +82,8 @@
     fetches[1].wait()
     count = cnt[...]
     slot = lax.broadcasted_iota(jnp.int32, (elems, unk), 0)
-    oldp[pl.ds(GROUP, elems)] = jnp.where(slot < count, old[0], 0.0)
+    live[...] = jnp.where(slot < count, 1.0, 0.0)
+    oldp[pl.ds(GROUP, elems)] = old[0] * live[...]
 
     pl.semaphore_wait(barrier, sum(there.astype(jnp.int32) for there, _ in neighbours))
 
@@ -126,7 +127,7 @@
     for i, index in enumerate((up, down)):
         local = (index[...] % GROUP).astype(jnp.float32)
         column = jnp.sum(jnp.where(diagonal, jnp.broadcast_to(local, square), 0.0), axis=1, keepdims=True)
-        rel[i] = jnp.broadcast_to(column, (elems, 128))
+        rel[i] = jnp.broadcast_to(column, (elems, unk))
 
     n2 = NVAR * NVAR
     entry = lax.broadcasted_iota(jnp.int32, (n2, NVAR * wide), 0)
@@ -146,7 +147,7 @@
     row = lax.broadcasted_iota(jnp.int32, (GROUP, unk), 0)
 
     def permuted(x, which, g):
-        column = rel[which, rows(g)][:, 0:1]
+        column = rel[which, rows(g)]
         out = jnp.broadcast_to(x[0:1], (GROUP, unk))
         for k in range(1, GROUP):
             out = jnp.where(column == float(k), x[k : k + 1], out)
@@ -172,7 +173,7 @@
                 flat, a_vm[j * GROUP + k], CONTRACT_LAST, preferred_element_type=jnp.float32
             )
             out = jnp.where(row == k, product, out)
-        return jnp.where(row + j * GROUP < count, out, 0.0)
+        return out * live[rows(j)]
 
     def prepare_forward():
         @pl.when(has_left)
@@ -370,7 +371,8 @@
             pltpu.VMEM((2 * blocks, GROUP, wide), f32),
             pltpu.VMEM((2 * blocks, GROUP, wide), f32),
             pltpu.VMEM((2, elems, unk), f32),
-            pltpu.VMEM((2, elems, 128), f32),
+            pltpu.VMEM((2, elems, unk), f32),
+            pltpu.VMEM((elems, unk), f32),
             pltpu.VMEM((GROUP, unk), f32),
             dma((7,)), dma((blocks + 1,)), dma((groups,)), dma, dma, dma((4,)), dma((4,)),
             dma((2 * blocks,)), dma((2 * blocks,)),

time: 82.3 us -> 80.2 us (0.974)
  Pallas kernels: 77.7 us -> 75.6 us
    pallas_call x1, Pallas kernels: 77.7 us -> 75.6 us  [per_device(): pl.pallas_call(functools.partial(sweep_kernel, nf, nc), out_shape=(jax.Sh...]
where the time goes in v7:
time: 80.2 us; the launch traced here: 80 us
  Pallas kernels  75.6 us (94%)
  local copies, waits for them, and re-layouts  3.08 us (4%)
  between operations  1.29 us (2%)
    pallas_call x1, Pallas kernels, per_device(): pl.pallas_call(functools.partial(sweep_kernel, nf, nc), out_shape=(jax.Sh...  75.6 us
    unnamed x2, local copies, waits for them, and re-layouts  3.08 us

profile of v7, /device:TPU:0, one launch (start us, length us, event | category | flops | bytes accessed | tf_op | source)
XLA Modules:
  0.0 80.0 jit_solution(4358034460829549461)
XLA Ops:
  1.3 75.6 %sweep.1 = (f32[1,64,320]{2,1,0:T(8,128)}, f32[1,64,320]{2,1,0:T(8,128)}) custom-call(f32[1,64,320]{2,1,0:T(8,128)} %rhs_hbm.1, f32[1,64,320]{2,1,0:T(8,128)} %old_hbm.1, bf16[1,64,320,320]{3,2,1,0:T(8,128)(2,1)} %ainv.1, f32[25,4,64]{2,1,0:T(4,128)} %bitcast.3, f32[4,64,64]{2,1,0:T(8,128)} %lift_hbm.1, s32[1,64]{1,0:T(1,128)} %up_hbm.1, s32[1,64]{1,0:T(1,128)} %down_hbm.1, ...), custom_call_target="tpu_custom_call" | custom-call | flops 26214400 | bytes 13107200 | tf_op jit(solution)/shard_map/sweep/pallas_call | solution.py:349
  76.9 1.5 %copy.13 = f32[1,64,320]{2,1,0:T(8,128)} copy(f32[1,64,320]{2,1,0:T(8,128)} %get-tuple-element.4) | data formatting | bytes 163840
  78.5 1.5 %copy.14 = f32[1,64,320]{2,1,0:T(8,128)} copy(f32[1,64,320]{2,1,0:T(8,128)} %get-tuple-element.5) | data formatting | bytes 163840

commit v8 on v7

--- a/solution.py
+++ b/solution.py
@@ -20,7 +20,7 @@
     rhs_hbm, old_hbm, ainv, jac_hbm, lift_hbm, up_hbm, down_hbm, cnt_hbm,
     half_hbm, full_hbm,
     rhs, old, jac, lift, up, down, cnt,
-    a_vm, jx, lt, oldp, result, down_in, halo, inbox, outbox, fix, rel, live, coupled_ref,
+    a_vm, jx, lt, oldp, result, down_in, halo, inbox, outbox, fix, rel, live, coupled_ref, packed,
     in_sem, out_sem, a_sem, old_send, old_recv, halo_send, halo_recv, box_send, box_recv,
 ):
     elems, unk = rhs.shape[1], rhs.shape[2]
@@ -29,6 +29,8 @@
     groups = elems // GROUP
     blocks = elems // GROUP
     halfp = result.at[0]
+    main = unk - unk // NVAR
+    rest = unk - main
     f = lax.axis_index("flow")
     c = lax.axis_index("cross")
     has_up, has_down = f > 0, f < nf - 1
@@ -166,14 +168,26 @@
         return total
 
     def solve(resid, j):
-        flat = resid.astype(jnp.bfloat16)
+        tail = jnp.concatenate([resid[:, main:]] * GROUP, axis=1)
+        lane = lax.broadcasted_iota(jnp.int32, (GROUP, GROUP * rest), 1)
+        line = lax.broadcasted_iota(jnp.int32, (GROUP, GROUP * rest), 0)
+        tail = jnp.where(lane // rest == line, tail, 0.0).astype(jnp.bfloat16)
+        head = resid[:, :main].astype(jnp.bfloat16)
         out = jnp.zeros((GROUP, unk), jnp.float32)
         for k in range(GROUP):
             product = lax.dot_general(
-                flat, a_vm[j * GROUP + k], CONTRACT_LAST, preferred_element_type=jnp.float32
+                head, a_vm[j * GROUP + k, :, 0:main], CONTRACT_LAST, preferred_element_type=jnp.float32
             )
             out = jnp.where(row == k, product, out)
+        out = out + lax.dot_general(tail, packed[j], CONTRACT_LAST, preferred_element_type=jnp.float32)
         return out * live[rows(j)]
+
+    def pack(j, carry):
+        a_copy(j).wait()
+        packed[j] = jnp.concatenate([a_vm[j * GROUP + k, :, main:] for k in range(GROUP)], axis=1)
+        return carry
+
+    lax.fori_loop(0, blocks, pack, 0)
 
     def prepare_forward():
         @pl.when(has_left)
@@ -266,10 +280,6 @@
         @pl.when(t == 2 * blocks - 1)
         def _():
             prepare_first_group()
-
-        @pl.when(forward)
-        def _():
-            a_copy(j).wait()
 
         @pl.when(jnp.logical_or(jnp.logical_and(forward, has_up), jnp.logical_and(backward, has_down)))
         def _():
@@ -374,6 +384,7 @@
             pltpu.VMEM((2, elems, unk), f32),
             pltpu.VMEM((elems, unk), f32),
             pltpu.VMEM((GROUP, unk), f32),
+            pltpu.VMEM((blocks, unk, GROUP * (unk // NVAR)), jnp.bfloat16),
             dma((7,)), dma((blocks + 1,)), dma((groups,)), dma, dma, dma((4,)), dma((4,)),
             dma((2 * blocks,)), dma((2 * blocks,)),
         ],

time: 80.2 us -> 76.8 us (0.958)
  Pallas kernels: 75.6 us -> 72.3 us
    pallas_call x1, Pallas kernels: 75.6 us -> 72.3 us  [per_device(): pl.pallas_call(functools.partial(sweep_kernel, nf, nc), out_shape=(jax.Sh...]
where the time goes in v8:
time: 76.8 us; the launch traced here: 76.7 us
  Pallas kernels  72.3 us (94%)
  local copies, waits for them, and re-layouts  3.08 us (4%)
  between operations  1.29 us (2%)
    pallas_call x1, Pallas kernels, per_device(): pl.pallas_call(functools.partial(sweep_kernel, nf, nc), out_shape=(jax.Sh...  72.3 us
    unnamed x2, local copies, waits for them, and re-layouts  3.08 us

profile of v8, /device:TPU:0, one launch (start us, length us, event | category | flops | bytes accessed | tf_op | source)
XLA Modules:
  0.0 76.7 jit_solution(8574728078945055051)
XLA Ops:
  1.3 72.3 %sweep.1 = (f32[1,64,320]{2,1,0:T(8,128)}, f32[1,64,320]{2,1,0:T(8,128)}) custom-call(f32[1,64,320]{2,1,0:T(8,128)} %rhs_hbm.1, f32[1,64,320]{2,1,0:T(8,128)} %old_hbm.1, bf16[1,64,320,320]{3,2,1,0:T(8,128)(2,1)} %ainv.1, f32[25,4,64]{2,1,0:T(4,128)} %bitcast.3, f32[4,64,64]{2,1,0:T(8,128)} %lift_hbm.1, s32[1,64]{1,0:T(1,128)} %up_hbm.1, s32[1,64]{1,0:T(1,128)} %down_hbm.1, ...), custom_call_target="tpu_custom_call" | custom-call | flops 26214400 | bytes 13107200 | tf_op jit(solution)/shard_map/sweep/pallas_call | solution.py:359
  73.6 1.5 %copy.13 = f32[1,64,320]{2,1,0:T(8,128)} copy(f32[1,64,320]{2,1,0:T(8,128)} %get-tuple-element.4) | data formatting | bytes 163840
  75.1 1.5 %copy.14 = f32[1,64,320]{2,1,0:T(8,128)} copy(f32[1,64,320]{2,1,0:T(8,128)} %get-tuple-element.5) | data formatting | bytes 163840
